TPU v7x, 256 devices: a whole 4x4x8 slice. The times are simulated.
256 devices in a mesh: lat: 16 (over y, x_hi, core), lon: 16 (over x_lo, z).
Axes of the slice: x: 4 (x_hi: 2, x_lo: 2; x = x_hi * 2 + x_lo), y: 4, z: 8, core: 2. Of those that a mesh axis runs over, the one named last changes fastest.
Arguments:
- features: bfloat16 [384, 720, 256], P('lat', 'lon'), may hold values from -6 to 6
- obs_mask: int32 [384, 720, 8], P('lat', 'lon'), may hold values 0 or 1
- filter_taps: bfloat16 [384, 4, 3, 17], replicated, may hold values from 0.049804688 to 1
- band_width: int32 [384], replicated, may hold values from 1 to 8, as said below
- mixing: bfloat16 [8, 4, 32, 32], replicated, may hold values from -0.5 to 0.5
- cotangent: bfloat16 [384, 720, 256], P('lat', 'lon'), may hold values from -6 to 6
Outputs:
- infilled: bfloat16 [384, 720, 256], P('lat', 'lon')
- input_grad: bfloat16 [384, 720, 256], P('lat', 'lon')
- weight_grad: float32 [8, 4, 32, 32], replicated
Inputs may be any that keep to these rules, and one draw needn't show every extreme that they name: band_width is 8 at the first and last cycle and 1 at cycle 384 // 2.
All inputs are finite; a program needn't handle non-finite values. No bound on the sum of `obs_mask` on one device may be relied on, other than what follows from the above.
Results may differ from a plain program's by a relative error of at most 0.005.
Values may be sent and summed in bfloat16 or wider, within the bound.
A program may use at most 128 MiB of HBM per device.

v0:
```python
import math

import jax
import jax.numpy as jnp
from jax import lax
from jax.sharding import PartitionSpec as P


def with_halo(block, sides, width, periodic):
    for axis, dim in sides:
        count = lax.axis_size(axis)
        forward = [(i, i + 1) for i in range(count - 1)]
        if periodic:
            forward.append((count - 1, 0))
        backward = [(target, source) for source, target in forward]
        low = lax.ppermute(
            lax.slice_in_dim(block, block.shape[dim] - width, None, axis=dim), axis, forward
        )
        high = lax.ppermute(lax.slice_in_dim(block, 0, width, axis=dim), axis, backward)
        block = jnp.concatenate([low, block, high], axis=dim)
    return block


def local(features, obs_mask, filter_taps, band_width, mixing, cotangent):
    row_count, col_count, chan_count = features.shape
    group_count = obs_mask.shape[2]
    group_width = chan_count // group_count
    basis_count = mixing.shape[1]
    tap_count = filter_taps.shape[3]
    tap_reach = (tap_count - 1) // 2
    padded_cols = col_count + 2 * tap_reach
    mask_values = obs_mask.astype(jnp.bfloat16)
    masked = (
        features.reshape(row_count, col_count, group_count, group_width) * mask_values[..., None]
    ).reshape(row_count, col_count, chan_count)
    wide_input, wide_mask = (
        with_halo(masked, (("lon", 1),), tap_reach, True),
        with_halo(mask_values, (("lon", 1),), tap_reach, True),
    )
    full_input, full_mask = (
        with_halo(wide_input, (("lat", 0),), 1, False),
        with_halo(wide_mask, (("lat", 0),), 1, False),
    )
    offsets = jnp.arange(tap_count) - tap_reach
    allowed = jnp.abs(offsets)[None, :] <= band_width[:, None]
    global_taps = filter_taps * allowed[:, None, None, :].astype(jnp.bfloat16)
    first_row = lax.axis_index("lat") * row_count
    local_taps = lax.dynamic_slice_in_dim(global_taps, first_row, row_count, 0)
    padded_index = jnp.arange(padded_cols)
    output_index = jnp.arange(col_count)
    tap_index = jnp.arange(tap_count)
    forward_table = (
        padded_index[None, :, None] - output_index[None, None, :] == tap_index[:, None, None]
    ).astype(jnp.bfloat16)
    band_blocks = jnp.einsum(
        "ibed,dpj->ibepj", local_taps, forward_table, preferred_element_type=jnp.float32
    ).astype(jnp.bfloat16)
    numerator = jnp.zeros((row_count, basis_count, col_count, chan_count), jnp.float32)
    denominator = jnp.zeros((row_count, basis_count, col_count, group_count), jnp.float32)
    for lat_step in range(3):
        band_block = band_blocks[:, :, lat_step]
        numerator = numerator + jnp.einsum(
            "ibpj,ipc->ibjc",
            band_block,
            full_input[lat_step : lat_step + row_count],
            preferred_element_type=jnp.float32,
        )
        denominator = denominator + jnp.einsum(
            "ibpj,ipg->ibjg",
            band_block,
            full_mask[lat_step : lat_step + row_count],
            preferred_element_type=jnp.float32,
        )
    safe_denom = jnp.maximum(denominator, 1.0)
    scaled = (
        numerator.reshape(row_count, basis_count, col_count, group_count, group_width)
        / safe_denom[..., None]
    ).astype(jnp.bfloat16)
    infilled = (
        jnp.einsum("ibjgc,gbco->ijgo", scaled, mixing, preferred_element_type=jnp.float32)
        .reshape(row_count, col_count, chan_count)
        .astype(jnp.bfloat16)
    )
    upstream = cotangent.reshape(row_count, col_count, group_count, group_width)
    local_grad = jnp.einsum(
        "ibjgc,ijgo->gbco", scaled, upstream, preferred_element_type=jnp.float32
    )
    cell_count = row_count * lax.axis_size("lat") * col_count * lax.axis_size("lon")
    weight_grad = lax.psum(local_grad, ("lat", "lon")) * (1.0 / math.sqrt(cell_count))
    back_prop = jnp.einsum("ijgo,gbco->ibjgc", upstream, mixing, preferred_element_type=jnp.float32)
    pulled = (
        (back_prop / safe_denom[..., None])
        .astype(jnp.bfloat16)
        .reshape(row_count, basis_count, col_count, chan_count)
    )
    wide_grad = with_halo(pulled, (("lon", 2),), tap_reach, True)
    full_grad = with_halo(wide_grad, (("lat", 0),), 1, False)
    padded_taps = jnp.pad(global_taps, ((1, 1), (0, 0), (0, 0), (0, 0)))
    nearby_taps = lax.dynamic_slice_in_dim(padded_taps, first_row, row_count + 2, 0)
    backward_table = (
        output_index[None, None, :] - padded_index[None, :, None] + 2 * tap_reach
        == tap_index[:, None, None]
    ).astype(jnp.bfloat16)
    adjoint_blocks = jnp.einsum(
        "ibed,dxl->ibexl", nearby_taps, backward_table, preferred_element_type=jnp.float32
    ).astype(jnp.bfloat16)
    gathered = jnp.zeros((row_count, col_count, chan_count), jnp.float32)
    for lat_step in range(3):
        start_row = 2 - lat_step
        gathered = gathered + jnp.einsum(
            "kbxl,kbxc->klc",
            adjoint_blocks[start_row : start_row + row_count, :, lat_step],
            full_grad[start_row : start_row + row_count],
            preferred_element_type=jnp.float32,
        )
    input_grad = (
        (gathered.reshape(row_count, col_count, group_count, group_width) * mask_values[..., None])
        .reshape(row_count, col_count, chan_count)
        .astype(jnp.bfloat16)
    )
    return (infilled, input_grad, weight_grad)


def solution(mesh):
    placed = (P("lat", "lon", None), P("lat", "lon", None), P(), P(), P(), P("lat", "lon", None))
    return jax.shard_map(
        local,
        mesh=mesh,
        in_specs=placed,
        out_specs=(P("lat", "lon", None), P("lat", "lon", None), P()),
        check_vma=False,
    )
```

profile of v0, /device:TPU:1, one launch (start us, length us, event | category | flops | bytes accessed | tf_op | source)
XLA Modules:
  0.0 431.0 jit_solution(16670597599679970714)
XLA Ops:
  7.2 0.9 convert_element_type.45
  8.9 2.5 collective-permute-start.4
  11.3 4.9 %collective-permute-start.5 = (bf16[24,8,8]{1,2,0:T(8,128)(2,1)}, bf16[24,8,8]{1,2,0:T(8,128)(2,1)S(1)}, u32[]{:S(2)}, u32[]{:S(2)}) collective-permute-start(bf16[24,8,8]{1,2,0:T(8,128)(2,1)} %get-tuple-element.29), channel_id=1, source_target_pairs={{1,0},{2,1},{3,2},{4,3},{5,4},{6,5},{7,6},{8,7},{9,8},{10,9},{11,1... | collective-permute-start | bytes 9224 | tf_op jit(solution)/shard_map/ppermute | solution.py:19
  16.5 1.4 mul.42
  17.8 1.5 mul.43
  19.4 1.3 copy_multiply_fusion
  21.4 3.6 collective-permute-start.1
  26.0 1.0 convolution_convert_fusion.1
  27.0 1.6 slice_bitcast_fusion.3
  28.6 1.3 convolution_convert_fusion
  29.9 3.0 slice_bitcast_fusion.2
  32.8 1.0 copy.85
  33.9 3.6 reshape.90
  37.5 4.9 %copy.102 = bf16[24,45,8,32,1]{1,3,0,4,2:T(8,128)(2,1)} copy(bf16[24,45,8,32,1]{3,2,0,1,4:T(8,128)(2,1)} %bitcast.129) | data formatting | bytes 1105920 | tf_op jit(solution)/shard_map/reshape | solution.py:84
  42.4 4.1 mul.45
  46.5 4.3 %mul.46 = f32[24,45,256]{2,0,1:T(8,128)} reshape(f32[24,45,8,32]{3,2,0,1:T(8,128)} %mul.45) | data formatting | bytes 2211840 | tf_op jit(solution)/shard_map/mul | solution.py:117
  51.0 5.9 %collective-permute-start.6 = (bf16[1,61,8]{1,2,0:T(8,128)(2,1)S(1)}, bf16[1,61,8]{1,2,0:T(8,128)(2,1)S(1)}, u32[]{:S(2)}, u32[]{:S(2)}) collective-permute-start(bf16[1,61,8]{1,2,0:T(8,128)(2,1)S(1)} %get-tuple-element.26), channel_id=1, source_target_pairs={{0,16},{16,32},{32,48},{48,64},{64,80},{80,96},{96,112},{112,128},... | collective-permute-start | bytes 2936 | tf_op jit(solution)/shard_map/ppermute | solution.py:16
  56.9 2.1 collective-permute-start.7
  59.1 1.2 fusion.32
  60.3 3.0 collective-permute-done.7
  63.3 1.2 fusion.26
  64.6 1.2 fusion.22
  66.1 3.7 fusion
  69.8 12.6 %copy.118 = bf16[24,4,45,8,32]{4,3,2,1,0:T(8,128)(2,1)} copy(bf16[24,4,45,8,32]{2,4,0,1,3:T(8,128)(2,1)} %fusion) | data formatting | bytes 4423680 | tf_op jit(solution)/shard_map/reshape | solution.py:94
  82.3 10.6 %reshape.112 = bf16[24,4,45,256]{3,2,1,0:T(8,128)(2,1)S(1)} reshape(bf16[24,4,45,8,32]{4,3,2,1,0:T(8,128)(2,1)} %copy.118) | data formatting | bytes 4423680 | tf_op jit(solution)/shard_map/reshape | solution.py:94
  92.9 1.0 fusion.74
  93.9 3.6 collective-permute-start.9
  97.6 1.9 collective-permute-start.3
  99.5 5.5 %collective-permute-start.2 = (bf16[1,61,256]{2,1,0:T(8,128)(2,1)S(1)}, bf16[1,61,256]{2,1,0:T(8,128)(2,1)S(1)}, u32[]{:S(2)}, u32[]{:S(2)}) collective-permute-start(bf16[1,61,256]{2,1,0:T(8,128)(2,1)S(1)} %get-tuple-element.23), channel_id=1, source_target_pairs={{0,16},{16,32},{32,48},{48,64},{64,80},{80,96},{96,112},{112,128},... | collective-permute-start | bytes 93704 | tf_op jit(solution)/shard_map/ppermute | solution.py:16
  105.1 0.8 fusion.34
  105.9 0.8 fusion.37
  107.3 3.0 add_add_fusion
  110.2 11.8 %reshape.111 = f32[24,4,45,8,32]{4,3,2,1,0:T(8,128)} reshape(f32[24,4,45,256]{3,2,1,0:T(8,128)} %add_add_fusion) | data formatting | bytes 8847360 | tf_op jit(solution)/shard_map/reshape | solution.py:76
  122.0 17.0 %copy.72 = f32[24,4,45,8,32]{2,4,0,1,3:T(8,128)} copy(f32[24,4,45,8,32]{4,3,2,1,0:T(8,128)} %reshape.111) | data formatting | bytes 8847360 | tf_op jit(solution)/shard_map/reshape | solution.py:76
  139.0 9.4 %divide_convert_fusion = bf16[24,4,45,8,32]{2,4,0,1,3:T(8,128)(2,1)} fusion(f32[24,4,45,8,32]{2,4,0,1,3:T(8,128)} %copy.72, f32[24,4,45,8]{2,0,1,3:T(8,128)S(1)} %copy-done.9), kind=kLoop, calls=%fused_computation.2 | loop fusion | flops 2211840 | bytes 6773760 | tf_op jit(solution)/shard_map/convert_element_type | solution.py:78
  148.4 5.8 %convolution_bitcast_fusion = f32[8,4,32,32]{3,2,1,0:T(8,128)} fusion(bf16[24,4,45,8,32]{2,4,0,1,3:T(8,128)(2,1)} %divide_convert_fusion, bf16[24,45,8,32,1]{1,3,0,4,2:T(8,128)(2,1)} %copy.102), kind=kOutput, calls=%fused_computation.31 | convolution fusion | flops 70778880 | bytes 2895872 | tf_op jit(solution)/shard_map/ibjgc,ijgo->gbco/dot_general | solution.py:85
  154.2 4.9 %fusion.11 = bf16[24,45,8,32]{1,3,0,2:T(8,128)(2,1)} fusion(bf16[24,4,45,8,32]{2,4,0,1,3:T(8,128)(2,1)} %divide_convert_fusion, bf16[8,4,32,32]{3,2,1,0:T(8,128)(2,1)S(1)} %copy-done), kind=kOutput, calls=%fused_computation.23 | convolution fusion | flops 71055360 | bytes 2830336 | tf_op jit(solution)/shard_map/ibjgc,gbco->ijgo/dot_general | solution.py:80
  159.1 5.8 %copy.75 = bf16[24,45,8,32]{3,2,0,1:T(8,128)(2,1)} copy(bf16[24,45,8,32]{1,3,0,2:T(8,128)(2,1)} %fusion.11) | data formatting | bytes 1105920 | tf_op jit(solution)/shard_map/convert_element_type | solution.py:82
  164.9 4.0 convert_element_type.49
  168.9 235.4 %all-reduce.3.cloned.1.call-done = f32[8,4,32,32]{3,2,1,0:T(8,128)} async-done(((f32[8,4,32,32]{3,2,1,0:T(8,128)}), f32[8,4,32,32]{3,2,1,0:T(8,128)}) %all-reduce.3.cloned.1.call-update) | async-done | bytes 131088 | tf_op jit(solution)/shard_map/psum | solution.py:89
  404.3 1.9 broadcast_multiply_fusion.1
  406.2 0.9 pad_maximum_fusion.36
  407.1 3.9 collective-permute-start.10
  411.0 4.9 %collective-permute-start.11 = (bf16[1,4,61,256]{3,2,1,0:T(8,128)(2,1)S(1)}, bf16[1,4,61,256]{3,2,1,0:T(8,128)(2,1)S(1)}, u32[]{:S(2)}, u32[]{:S(2)}) collective-permute-start(bf16[1,4,61,256]{3,2,1,0:T(8,128)(2,1)S(1)} %get-tuple-element.19), channel_id=1, source_target_pairs={{0,16},{16,32},{32,48},{48,64},{64,80},{80,96},{96,112},{112,128},... | collective-permute-start | bytes 374792 | tf_op jit(solution)/shard_map/ppermute | solution.py:16
  416.0 1.9 fusion.12
  417.9 3.1 fusion.16
  421.1 2.1 fusion.20
  423.2 1.0 copy.88
  (62 shorter events, 3.9 us)
Async XLA Ops:
  7.2 58.9 %copy-start = (bf16[8,4,32,32]{3,2,1,0:T(8,128)(2,1)S(1)}, bf16[8,4,32,32]{3,2,1,0:T(8,128)(2,1)}, u32[]{:S(2)}) copy-start(bf16[8,4,32,32]{3,2,1,0:T(8,128)(2,1)} %param.10) | copy-start | bytes 196612
  7.2 397.1 %all-reduce.3.cloned.1.call-start = ((), (), s32[]{:S(2)}) async-start(), calls=%async_computation | async-start | bytes 1048576 | tf_op jit(solution)/shard_map/psum | solution.py:89
  8.9 42.0 %collective-permute-start.4 = (bf16[24,8,8]{1,2,0:T(8,128)(2,1)}, bf16[24,8,8]{1,2,0:T(8,128)(2,1)S(1)}, u32[]{:S(2)}, u32[]{:S(2)}) collective-permute-start(bf16[24,8,8]{1,2,0:T(8,128)(2,1)} %get-tuple-element.28), channel_id=1, source_target_pairs={{0,1},{1,2},{2,3},{3,4},{4,5},{5,6},{6,7},{7,8},{8,9},{9,10},{10,1... | collective-permute-start | bytes 9224 | tf_op jit(solution)/shard_map/ppermute | solution.py:16
  11.3 39.5 %collective-permute-start.5 = (bf16[24,8,8]{1,2,0:T(8,128)(2,1)}, bf16[24,8,8]{1,2,0:T(8,128)(2,1)S(1)}, u32[]{:S(2)}, u32[]{:S(2)}) collective-permute-start(bf16[24,8,8]{1,2,0:T(8,128)(2,1)} %get-tuple-element.29), channel_id=1, source_target_pairs={{1,0},{2,1},{3,2},{4,3},{5,4},{6,5},{7,6},{8,7},{9,8},{10,9},{11,1... | collective-permute-start | bytes 9224 | tf_op jit(solution)/shard_map/ppermute | solution.py:19
  19.4 5.6 %copy-start.15 = (s32[384]{0:T(512)S(1)}, s32[384]{0:T(512)}, u32[]{:S(2)}) copy-start(s32[384]{0:T(512)} %param.9) | copy-start | bytes 4612
  19.4 5.8 %copy-start.14 = (bf16[384,4,3,17]{0,1,3,2:T(4,128)(2,1)S(1)}, bf16[384,4,3,17]{0,1,3,2:T(4,128)(2,1)}, u32[]{:S(2)}) copy-start(bf16[384,4,3,17]{0,1,3,2:T(4,128)(2,1)} %param.8) | copy-start | bytes 470020
  21.4 76.1 %collective-permute-start = (bf16[24,8,256]{2,1,0:T(8,128)(2,1)}, bf16[24,8,256]{2,1,0:T(8,128)(2,1)S(1)}, u32[]{:S(2)}, u32[]{:S(2)}) collective-permute-start(bf16[24,8,256]{2,1,0:T(8,128)(2,1)} %get-tuple-element.24), channel_id=1, source_target_pairs={{0,1},{1,2},{2,3},{3,4},{4,5},{5,6},{6,7},{7,8},{8,9},{9,10},{10,1... | collective-permute-start | bytes 294920 | tf_op jit(solution)/shard_map/ppermute | solution.py:16
  21.4 76.1 %collective-permute-start.1 = (bf16[24,8,256]{2,1,0:T(8,128)(2,1)}, bf16[24,8,256]{2,1,0:T(8,128)(2,1)S(1)}, u32[]{:S(2)}, u32[]{:S(2)}) collective-permute-start(bf16[24,8,256]{2,1,0:T(8,128)(2,1)} %get-tuple-element.25), channel_id=1, source_target_pairs={{1,0},{2,1},{3,2},{4,3},{5,4},{6,5},{7,6},{8,7},{9,8},{10,9},{11,1... | collective-permute-start | bytes 294920 | tf_op jit(solution)/shard_map/ppermute | solution.py:19
  28.6 30.5 %copy-start.3 = (bf16[24,4,61,45]{2,0,3,1:T(8,128)(2,1)}, bf16[24,4,61,45]{2,0,3,1:T(8,128)(2,1)S(1)}, u32[]{:S(2)}) copy-start(bf16[24,4,61,45]{2,0,3,1:T(8,128)(2,1)S(1)} %get-tuple-element.16) | copy-start | bytes 1581124
  28.6 36.0 %copy-start.1 = (bf16[24,4,61,45]{2,0,3,1:T(8,128)(2,1)}, bf16[24,4,61,45]{2,0,3,1:T(8,128)(2,1)S(1)}, u32[]{:S(2)}) copy-start(bf16[24,4,61,45]{2,0,3,1:T(8,128)(2,1)S(1)} %get-tuple-element.17) | copy-start | bytes 1581124
  50.9 12.4 %copy-start.5 = (bf16[24,4,61,45]{2,0,3,1:T(8,128)(2,1)S(1)}, bf16[24,4,61,45]{2,0,3,1:T(8,128)(2,1)}, u32[]{:S(2)}) copy-start(bf16[24,4,61,45]{2,0,3,1:T(8,128)(2,1)} %get-tuple-element.15) | copy-start | bytes 1581124
  51.0 13.5 %collective-permute-start.6 = (bf16[1,61,8]{1,2,0:T(8,128)(2,1)S(1)}, bf16[1,61,8]{1,2,0:T(8,128)(2,1)S(1)}, u32[]{:S(2)}, u32[]{:S(2)}) collective-permute-start(bf16[1,61,8]{1,2,0:T(8,128)(2,1)S(1)} %get-tuple-element.26), channel_id=1, source_target_pairs={{0,16},{16,32},{32,48},{48,64},{64,80},{80,96},{96,112},{112,128},... | collective-permute-start | bytes 2936 | tf_op jit(solution)/shard_map/ppermute | solution.py:16
  56.9 6.4 %collective-permute-start.7 = (bf16[1,61,8]{1,2,0:T(8,128)(2,1)S(1)}, bf16[1,61,8]{1,2,0:T(8,128)(2,1)S(1)}, u32[]{:S(2)}, u32[]{:S(2)}) collective-permute-start(bf16[1,61,8]{1,2,0:T(8,128)(2,1)S(1)} %get-tuple-element.27), channel_id=1, source_target_pairs={{16,0},{32,16},{48,32},{64,48},{80,64},{96,80},{112,96},{128,112},... | collective-permute-start | bytes 2936 | tf_op jit(solution)/shard_map/ppermute | solution.py:19
  64.5 1.5 copy-start.7
  66.1 3.7 copy-start.8
  92.9 12.2 %copy-start.4 = (bf16[24,4,61,45]{2,0,3,1:T(8,128)(2,1)S(1)}, bf16[24,4,61,45]{2,0,3,1:T(8,128)(2,1)}, u32[]{:S(2)}) copy-start(bf16[24,4,61,45]{2,0,3,1:T(8,128)(2,1)} %copy-done.3) | copy-start | bytes 1581124
  93.9 312.3 %collective-permute-start.8 = (bf16[24,4,8,256]{3,2,1,0:T(8,128)(2,1)}, bf16[24,4,8,256]{3,2,1,0:T(8,128)(2,1)}, u32[]{:S(2)}, u32[]{:S(2)}) collective-permute-start(bf16[24,4,8,256]{3,2,1,0:T(8,128)(2,1)} %get-tuple-element.20), channel_id=1, source_target_pairs={{0,1},{1,2},{2,3},{3,4},{4,5},{5,6},{6,7},{7,8},{8,9},{9,10},{10,1... | collective-permute-start | bytes 1179656 | tf_op jit(solution)/shard_map/ppermute | solution.py:16
  93.9 312.3 %collective-permute-start.9 = (bf16[24,4,8,256]{3,2,1,0:T(8,128)(2,1)}, bf16[24,4,8,256]{3,2,1,0:T(8,128)(2,1)}, u32[]{:S(2)}, u32[]{:S(2)}) collective-permute-start(bf16[24,4,8,256]{3,2,1,0:T(8,128)(2,1)} %get-tuple-element.21), channel_id=1, source_target_pairs={{1,0},{2,1},{3,2},{4,3},{5,4},{6,5},{7,6},{8,7},{9,8},{10,9},{11,1... | collective-permute-start | bytes 1179656 | tf_op jit(solution)/shard_map/ppermute | solution.py:19
  97.6 9.7 %collective-permute-start.3 = (bf16[1,61,256]{2,1,0:T(8,128)(2,1)S(1)}, bf16[1,61,256]{2,1,0:T(8,128)(2,1)S(1)}, u32[]{:S(2)}, u32[]{:S(2)}) collective-permute-start(bf16[1,61,256]{2,1,0:T(8,128)(2,1)S(1)} %get-tuple-element.22), channel_id=1, source_target_pairs={{16,0},{32,16},{48,32},{64,48},{80,64},{96,80},{112,96},{128,112},... | collective-permute-start | bytes 93704 | tf_op jit(solution)/shard_map/ppermute | solution.py:19
  99.5 6.4 %copy-start.2 = (bf16[24,4,61,45]{2,0,3,1:T(8,128)(2,1)S(1)}, bf16[24,4,61,45]{2,0,3,1:T(8,128)(2,1)}, u32[]{:S(2)}) copy-start(bf16[24,4,61,45]{2,0,3,1:T(8,128)(2,1)} %copy-done.1) | copy-start | bytes 1581124
  99.5 6.3 %collective-permute-start.2 = (bf16[1,61,256]{2,1,0:T(8,128)(2,1)S(1)}, bf16[1,61,256]{2,1,0:T(8,128)(2,1)S(1)}, u32[]{:S(2)}, u32[]{:S(2)}) collective-permute-start(bf16[1,61,256]{2,1,0:T(8,128)(2,1)S(1)} %get-tuple-element.23), channel_id=1, source_target_pairs={{0,16},{16,32},{32,48},{48,64},{64,80},{80,96},{96,112},{112,128},... | collective-permute-start | bytes 93704 | tf_op jit(solution)/shard_map/ppermute | solution.py:16
  105.8 1.4 copy-start.6
  122.0 17.0 %copy-start.9 = (f32[24,4,45,8]{2,0,1,3:T(8,128)S(1)}, f32[24,4,45,8]{2,0,1,3:T(8,128)}, u32[]{:S(2)}) copy-start(f32[24,4,45,8]{2,0,1,3:T(8,128)} %copy-done.8) | copy-start | bytes 414724
  406.2 9.8 %copy-start.12 = (bf16[24,4,61,45]{2,0,3,1:T(8,128)(2,1)S(1)}, bf16[24,4,61,45]{2,0,3,1:T(8,128)(2,1)}, u32[]{:S(2)}) copy-start(bf16[24,4,61,45]{2,0,3,1:T(8,128)(2,1)} %get-tuple-element.14) | copy-start | bytes 1581124
  407.1 14.0 %collective-permute-start.10 = (bf16[1,4,61,256]{3,2,1,0:T(8,128)(2,1)S(1)}, bf16[1,4,61,256]{3,2,1,0:T(8,128)(2,1)S(1)}, u32[]{:S(2)}, u32[]{:S(2)}) collective-permute-start(bf16[1,4,61,256]{3,2,1,0:T(8,128)(2,1)S(1)} %get-tuple-element.18), channel_id=1, source_target_pairs={{16,0},{32,16},{48,32},{64,48},{80,64},{96,80},{112,96},{128,112},... | collective-permute-start | bytes 374792 | tf_op jit(solution)/shard_map/ppermute | solution.py:19
  411.0 6.9 %collective-permute-start.11 = (bf16[1,4,61,256]{3,2,1,0:T(8,128)(2,1)S(1)}, bf16[1,4,61,256]{3,2,1,0:T(8,128)(2,1)S(1)}, u32[]{:S(2)}, u32[]{:S(2)}) collective-permute-start(bf16[1,4,61,256]{3,2,1,0:T(8,128)(2,1)S(1)} %get-tuple-element.19), channel_id=1, source_target_pairs={{0,16},{16,32},{32,48},{48,64},{64,80},{80,96},{96,112},{112,128},... | collective-permute-start | bytes 374792 | tf_op jit(solution)/shard_map/ppermute | solution.py:16
  416.0 1.9 copy-start.11
  417.9 3.2 copy-start.10
  417.9 3.2 copy-start.13
Sparse Core Ops, SparseCore 0:
  154.3 249.9 all-reduce.2
where the time goes:
time: 435 us; the launch traced here: 431 us
  waiting for transfers between devices  239 us (55%)
  local copies, waits for them, and re-layouts  91.8 us (21%)
  starting transfers between devices  38.9 us (9%)
  matrix products  32 us (7%)
  other arithmetic  14.7 us (3%)
  between operations  14.5 us (3%)
    psum x1, waiting for transfers between devices, local(): lax.psum(local_grad, ('lat', 'lon')) * (1.0 / math.sqrt(cell_count))  235 us
    reshape x2, local copies, waits for them, and re-layouts, local(): numerator.reshape(row_count, basis_count, col_count, group_count, group_w...  28.8 us
    reshape x2, local copies, waits for them, and re-layouts, local(): pulled = (back_prop / safe_denom[..., None]).astype(jnp.bfloat16).reshape...  23.1 us
    ppermute x6, starting transfers between devices, with_halo(): lax.ppermute(lax.slice_in_dim(block, 0, width, axis=dim), axis, backward)  20 us
    ppermute x6, starting transfers between devices, with_halo(): lax.ppermute(lax.slice_in_dim(block, block.shape[dim] - width, None, axis...  18.8 us
    convert_element_type x2, local copies, waits for them, and re-layouts, local(): infilled = jnp.einsum('ibjgc,gbco->ijgo', scaled, mixing, preferred_eleme...  9.73 us
    convert_element_type x1, other arithmetic, local(): scaled = (numerator.reshape(row_count, basis_count, col_count, group_coun...  9.37 us
  transfers between devices with their start and end apart: 13, of which 3 were waited for; matrix products, arithmetic and copies ran while one was open for 31% of the time, Pallas kernels for 0%

commit v1 on v0

v1 whole, which is shorter than its diff:
```python
import functools
import math

import jax
import jax.numpy as jnp
from jax import lax
from jax.experimental import pallas as pl
from jax.experimental.pallas import tpu as pltpu
from jax.sharding import PartitionSpec as P

MESH = pl.DeviceIdType.MESH
F32 = jnp.float32
BF16 = jnp.bfloat16
ROWS = 24
COLS = 45
PADC = 48
SLOT = 64
CHAN = 256
GROUPS = 8
WIDTH = 32
BASES = 4
REACH = 8
TAPS = 2 * REACH + 1
PAIRS = ROWS // 2
BAND = 2 * BASES * PADC


def iota(shape, dim):
    return lax.broadcasted_iota(jnp.int32, shape, dim)


def one_hot(test):
    return jnp.where(test, 1.0, 0.0).astype(BF16)


def dot(a, b):
    return jnp.dot(a, b, preferred_element_type=F32)


def pad_rows(x):
    return jnp.concatenate([x, jnp.zeros((PADC - COLS, x.shape[1]), F32)], axis=0)


def kernel(
    n_lat, n_lon,
    feat, mask, base, mix, cot,
    infilled, input_grad, weight_grad,
    field, seen, cots, cots_t, mixer, band, band_t, scaled, pulled, back, total,
    send_first, send_last, from_right, from_left, corners,
    share, got_lon, got_lat, final,
    part_right, part_left, part_top, part_bottom, part_corner,
    halo_send, halo_recv, part_send, part_recv, sum_send, sum_recv,
):
    la, lo = lax.axis_index("lat"), lax.axis_index("lon")
    up, down = lax.rem(la + n_lat - 1, n_lat), lax.rem(la + 1, n_lat)
    left, right = lax.rem(lo + n_lon - 1, n_lon), lax.rem(lo + 1, n_lon)

    barrier = pltpu.get_barrier_semaphore()

    def greet(dev_lat, dev_lon):
        pl.semaphore_signal(
            barrier, inc=1, device_id=(dev_lat, dev_lon), device_id_type=MESH
        )

    @pl.loop(1, n_lon)
    def _(d):
        greet(la, lax.rem(lo + d, n_lon))

    @pl.loop(1, n_lat)
    def _(d):
        greet(lax.rem(la + d, n_lat), lo)

    for dev_lat in (up, down):
        for dev_lon in (left, right):
            greet(dev_lat, dev_lon)

    expand = one_hot(iota((GROUPS, CHAN), 1) // WIDTH == iota((GROUPS, CHAN), 0))
    squeeze = one_hot(iota((CHAN, 128), 0) == WIDTH * iota((CHAN, 128), 1))
    expand_wide = one_hot(iota((128, CHAN), 1) // WIDTH == iota((128, CHAN), 0))

    @pl.loop(0, PAIRS)
    def _(t):
        firsts, lasts, first_seen, last_seen = [], [], [], []
        for k in range(2):
            i = 2 * t + k
            spread = dot(mask[i].astype(F32).astype(BF16), expand)
            masked = pad_rows(feat[i].astype(F32) * spread)
            spread = pad_rows(spread)
            field[i + 1, 0:PADC] = masked.astype(BF16)
            seen[i + 1, 0:PADC] = spread.astype(BF16)
            firsts.append(masked[0:8])
            first_seen.append(spread[0:8])
            lasts.append(pltpu.roll(masked[32:48], 11, 0)[0:8])
            last_seen.append(pltpu.roll(spread[32:48], 11, 0)[0:8])
        for ref, values, flags in (
            (send_first, firsts, first_seen), (send_last, lasts, last_seen)
        ):
            ref[t, :, 0:CHAN] = jnp.concatenate(values, axis=0).astype(BF16)
            marks = dot(jnp.concatenate(flags, axis=0).astype(BF16), squeeze)
            ref[t, :, CHAN:] = marks.astype(BF16)

    pl.semaphore_wait(barrier, n_lon - 1 + n_lat - 1 + 4)

    def remote(src, dst, send, recv, dev_lat, dev_lon):
        return pltpu.make_async_remote_copy(
            src_ref=src, dst_ref=dst, send_sem=send, recv_sem=recv,
            device_id=(dev_lat, dev_lon), device_id_type=MESH,
        )

    halo_plan = (
        (send_first, from_right, la, left),
        (send_last, from_left, la, right),
        (field.at[1, pl.ds(0, PADC)], field.at[ROWS + 1, pl.ds(0, PADC)], up, lo),
        (seen.at[1, pl.ds(0, PADC)], seen.at[ROWS + 1, pl.ds(0, PADC)], up, lo),
        (field.at[ROWS, pl.ds(0, PADC)], field.at[0, pl.ds(0, PADC)], down, lo),
        (seen.at[ROWS, pl.ds(0, PADC)], seen.at[0, pl.ds(0, PADC)], down, lo),
        (send_first.at[0], corners.at[0], up, left),
        (send_last.at[0], corners.at[1], up, right),
        (send_first.at[PAIRS - 1], corners.at[2], down, left),
        (send_last.at[PAIRS - 1], corners.at[3], down, right),
    )
    halos = [
        remote(src, dst, halo_send.at[n], halo_recv.at[n], dev_lat, dev_lon)
        for n, (src, dst, dev_lat, dev_lon) in enumerate(halo_plan)
    ]
    for copy in halos:
        copy.start()

    lane = iota((PADC, 128), 1) % SLOT

    @pl.loop(0, PAIRS)
    def _(t):
        for k in range(2):
            taps = base[2 * t + k]
            for b in range(BASES):
                for v in range(2):
                    line = taps[b : b + 1, v * 128 : v * 128 + 128]
                    row = jnp.broadcast_to(line, (PADC, 128))
                    late = pltpu.roll(jnp.broadcast_to(line, (8, 128)), 3, 1)
                    late = jnp.concatenate([late, late], axis=0)
                    own = pltpu.roll(row, 120, 1, stride=1, stride_axis=0)
                    high = pltpu.roll(late, 24, 1, stride=1, stride_axis=0)
                    low = pltpu.roll(row[0:8], 56, 1, stride=1, stride_axis=0)
                    piece = jnp.concatenate(
                        [
                            jnp.where(
                                lane[0:8] < COLS, own[0:8], jnp.where(lane[0:8] < 56, 0.0, low)
                            ),
                            own[8:32],
                            jnp.where(
                                lane[0:16] < COLS,
                                own[32:48],
                                jnp.where(
                                    (lane[0:16] >= PADC) & (lane[0:16] < 56), high, 0.0
                                ),
                            ),
                        ],
                        axis=0,
                    )
                    start = (k * BASES + b) * PADC
                    band[t, start : start + PADC, v * 128 : v * 128 + 128] = piece.astype(BF16)
        band_t[t] = band[t].T

    repeat = one_hot(iota((WIDTH, CHAN), 1) % WIDTH == iota((WIDTH, CHAN), 0))
    block = iota((CHAN, CHAN), 0) // WIDTH == iota((CHAN, CHAN), 1) // WIDTH
    for b in range(BASES):
        tall = mix[:, b].reshape(CHAN, WIDTH)
        mixer[b] = jnp.where(block, dot(tall, repeat), 0.0).astype(BF16)

    @pl.loop(0, ROWS)
    def _(i):
        start = pl.multiple_of(i * PADC, PADC)
        cots[pl.ds(start, PADC)] = pad_rows(cot[i].astype(F32)).astype(BF16)

    for n in range(ROWS * PADC // 128):
        cots_t[:, n * 128 : n * 128 + 128] = cots[n * 128 : n * 128 + 128].T

    @pl.loop(0, PAIRS // 4)
    def _(n):
        start = pl.multiple_of(n * 8 * PADC, 8 * PADC)
        rows = cots[pl.ds(start, 8 * PADC)]
        for b in range(BASES):
            result = lax.dot_general(
                rows, mixer[b], (((1,), (1,)), ((), ())), preferred_element_type=F32
            )
            for i in range(8):
                first = ((i % 2) * BASES + b) * PADC
                back[4 * n + i // 2, first : first + PADC] = result[i * PADC : i * PADC + PADC]

    for copy in halos:
        copy.wait_recv()

    def place(ref, i, high, low):
        ref[i, PADC:SLOT] = jnp.concatenate([high, low], axis=0).astype(BF16)

    def opened(strip):
        return strip[:, 0:CHAN].astype(F32), dot(strip[:, CHAN:], expand_wide)

    @pl.loop(0, PAIRS)
    def _(t):
        high, low = opened(from_right[t]), opened(from_left[t])
        for ref, h, l in zip((field, seen), high, low):
            place(ref, 2 * t + 1, h[0:8], l[0:8])
            place(ref, 2 * t + 2, h[8:16], l[8:16])

    for i, h_slot, l_slot, rows in ((ROWS + 1, 0, 1, slice(0, 8)), (0, 2, 3, slice(8, 16))):
        for ref, h, l in zip((field, seen), opened(corners[h_slot]), opened(corners[l_slot])):
            place(ref, i, h[rows], l[rows])

    @pl.loop(0, PAIRS)
    def _(t):
        weights = band[t]
        numerator = dot(weights, field[pl.ds(2 * t, 4)].reshape(4 * SLOT, CHAN))
        denominator = dot(weights, seen[pl.ds(2 * t, 4)].reshape(4 * SLOT, CHAN))
        inverse = 1.0 / jnp.maximum(denominator, 1.0)
        normal = (numerator * inverse).astype(BF16)
        for k in range(2):
            start = pl.multiple_of((2 * t + k) * PADC, PADC)
            for b in range(BASES):
                first = (k * BASES + b) * PADC
                scaled[b, pl.ds(start, PADC)] = normal[first : first + PADC]
        pulled[t] = (back[t] * inverse).astype(BF16)

    for b in range(BASES):
        grad = jnp.where(block, dot(cots_t[...], scaled[b]), 0.0)
        share[b * WIDTH : b * WIDTH + WIDTH] = jnp.sum(grad.reshape(GROUPS, WIDTH, CHAN), axis=0)

    def lon_share(d):
        to = lax.rem(lo + d, n_lon)
        rows = pl.ds(pl.multiple_of(to * 8, 8), 8)
        return remote(
            share.at[rows], got_lon.at[d], sum_send.at[0, d], sum_recv.at[0, d], la, to
        )

    def lat_share(d):
        to = lax.rem(la + d, n_lat)
        return remote(
            got_lat.at[la], got_lat.at[la], sum_send.at[1, d], sum_recv.at[1, d], to, lo
        )

    def spread_share(d):
        to = lax.rem(lo + d, n_lon)
        return remote(
            final.at[lo], final.at[lo], sum_send.at[2, d], sum_recv.at[2, d], la, to
        )

    def start_all(make, count):
        @pl.loop(1, count)
        def _(d):
            make(d).start()

    def finish_all(make, count):
        @pl.loop(1, count)
        def _(d):
            make(d).wait_recv()

        @pl.loop(1, count)
        def _(d):
            make(d).wait_send()

    start_all(lon_share, n_lon)

    @pl.loop(0, PAIRS // 4)
    def _(n):
        start = pl.multiple_of(n * 8 * PADC, 8 * PADC)
        result = dot(scaled[0, pl.ds(start, 8 * PADC)], mixer[0])
        for b in range(1, BASES):
            result += dot(scaled[b, pl.ds(start, 8 * PADC)], mixer[b])
        for i in range(8):
            infilled[8 * n + i] = result[i * PADC : i * PADC + COLS].astype(BF16)

    finish_all(lon_share, n_lon)
    got_lon[0] = share[pl.ds(pl.multiple_of(lo * 8, 8), 8)]
    got_lat[la] = jnp.sum(got_lon[...], axis=0)
    start_all(lat_share, n_lat)

    total[0:2] = jnp.zeros((2, SLOT, CHAN), F32)

    @pl.loop(0, PAIRS)
    def _(t):
        result = dot(band_t[t], pulled[t]).reshape(4, SLOT, CHAN)
        total[pl.ds(2 * t, 2)] += result[0:2]
        total[pl.ds(2 * t + 2, 2)] = result[2:4]

    inner = pl.ds(1, ROWS)
    high, low, own = pl.ds(PADC, 8), pl.ds(56, 8), pl.ds(0, PADC)
    part_plan = (
        (total.at[inner, low], part_right, la, left),
        (total.at[inner, high], part_left, la, right),
        (total.at[0, own], part_bottom, up, lo),
        (total.at[ROWS + 1, own], part_top, down, lo),
        (total.at[0, low], part_corner.at[0], up, left),
        (total.at[0, high], part_corner.at[1], up, right),
        (total.at[ROWS + 1, low], part_corner.at[2], down, left),
        (total.at[ROWS + 1, high], part_corner.at[3], down, right),
    )
    parts = [
        remote(src, dst, part_send.at[n], part_recv.at[n], dev_lat, dev_lon)
        for n, (src, dst, dev_lat, dev_lon) in enumerate(part_plan)
    ]
    for copy in parts:
        copy.start()

    finish_all(lat_share, n_lat)
    final[lo] = jnp.sum(got_lat[...], axis=0) * (
        1.0 / math.sqrt(ROWS * n_lat * COLS * n_lon)
    )
    start_all(spread_share, n_lon)

    for copy in parts:
        copy.wait_recv()
    for copy in parts:
        copy.wait_send()

    part_left[0] += part_corner[3]
    part_right[0] += part_corner[2]
    part_left[ROWS - 1] += part_corner[1]
    part_right[ROWS - 1] += part_corner[0]
    total[1, 0:PADC] += part_top[...]
    total[ROWS, 0:PADC] += part_bottom[...]

    @pl.loop(0, ROWS)
    def _(i):
        tail = pltpu.roll(
            jnp.concatenate([part_right[i], jnp.zeros((8, CHAN), F32)], axis=0), 5, 0
        )
        extra = jnp.concatenate([part_left[i], jnp.zeros((24, CHAN), F32), tail], axis=0)
        result = (total[i + 1, 0:PADC] + extra) * seen[i + 1, 0:PADC].astype(F32)
        input_grad[i] = result[0:COLS].astype(BF16)

    for copy in halos:
        copy.wait_send()
    finish_all(spread_share, n_lon)
    for b in range(BASES):
        grad = final[4 * b : 4 * b + 4].reshape(WIDTH, CHAN)
        weight_grad[:, b] = grad.T.reshape(GROUPS, WIDTH, WIDTH)


def local(features, obs_mask, filter_taps, band_width, mixing, cotangent):
    n_lat, n_lon = lax.axis_size("lat"), lax.axis_size("lon")
    first = lax.axis_index("lat") * ROWS
    taps = lax.dynamic_slice_in_dim(filter_taps, first, ROWS, 0).astype(F32)
    width = lax.dynamic_slice_in_dim(band_width, first, ROWS, 0)
    inside = jnp.abs(jnp.arange(TAPS) - REACH)[None, :] <= width[:, None]
    cycle = first + jnp.arange(ROWS)[:, None] + jnp.arange(3)[None, :] - 1
    on_sphere = (cycle >= 0) & (cycle < n_lat * ROWS)
    keep = inside[:, None, None, :] & on_sphere[:, None, :, None]
    taps = jnp.where(keep, taps, 0.0)
    taps = jnp.pad(taps, ((0, 0), (0, 0), (0, 0), (0, SLOT - TAPS)))
    taps = taps.reshape(PAIRS, 2, BASES, 3 * SLOT)
    base = jnp.stack(
        [
            jnp.pad(taps[:, 0], ((0, 0), (0, 0), (0, SLOT))),
            jnp.pad(taps[:, 1], ((0, 0), (0, 0), (SLOT, 0))),
        ],
        axis=1,
    ).reshape(ROWS, BASES, 4 * SLOT)

    vmem = pl.BlockSpec(memory_space=pltpu.VMEM)
    return pl.pallas_call(
        functools.partial(kernel, n_lat, n_lon),
        out_shape=(
            jax.ShapeDtypeStruct((ROWS, COLS, CHAN), BF16),
            jax.ShapeDtypeStruct((ROWS, COLS, CHAN), BF16),
            jax.ShapeDtypeStruct((GROUPS, BASES, WIDTH, WIDTH), F32),
        ),
        in_specs=[vmem] * 5,
        out_specs=(vmem,) * 3,
        scratch_shapes=[
            pltpu.VMEM((ROWS + 2, SLOT, CHAN), BF16),
            pltpu.VMEM((ROWS + 2, SLOT, CHAN), BF16),
            pltpu.VMEM((ROWS * PADC, CHAN), BF16),
            pltpu.VMEM((CHAN, ROWS * PADC), BF16),
            pltpu.VMEM((BASES, CHAN, CHAN), BF16),
            pltpu.VMEM((PAIRS, BAND, 4 * SLOT), BF16),
            pltpu.VMEM((PAIRS, 4 * SLOT, BAND), BF16),
            pltpu.VMEM((BASES, ROWS * PADC, CHAN), BF16),
            pltpu.VMEM((PAIRS, BAND, CHAN), BF16),
            pltpu.VMEM((PAIRS, BAND, CHAN), F32),
            pltpu.VMEM((ROWS + 2, SLOT, CHAN), F32),
            pltpu.VMEM((PAIRS, 16, CHAN + 128), BF16),
            pltpu.VMEM((PAIRS, 16, CHAN + 128), BF16),
            pltpu.VMEM((PAIRS, 16, CHAN + 128), BF16),
            pltpu.VMEM((PAIRS, 16, CHAN + 128), BF16),
            pltpu.VMEM((4, 16, CHAN + 128), BF16),
            pltpu.VMEM((BASES * WIDTH, CHAN), F32),
            pltpu.VMEM((16, 8, CHAN), F32),
            pltpu.VMEM((16, 8, CHAN), F32),
            pltpu.VMEM((16, 8, CHAN), F32),
            pltpu.VMEM((ROWS, 8, CHAN), F32),
            pltpu.VMEM((ROWS, 8, CHAN), F32),
            pltpu.VMEM((PADC, CHAN), F32),
            pltpu.VMEM((PADC, CHAN), F32),
            pltpu.VMEM((4, 8, CHAN), F32),
            pltpu.SemaphoreType.DMA((10,)),
            pltpu.SemaphoreType.DMA((10,)),
            pltpu.SemaphoreType.DMA((8,)),
            pltpu.SemaphoreType.DMA((8,)),
            pltpu.SemaphoreType.DMA((3, 16)),
            pltpu.SemaphoreType.DMA((3, 16)),
        ],
        compiler_params=pltpu.CompilerParams(
            collective_id=0, has_side_effects=True, vmem_limit_bytes=50 * 1024 * 1024
        ),
    )(features, obs_mask, base, mixing, cotangent)


def solution(mesh):
    placed = (P("lat", "lon", None), P("lat", "lon", None), P(), P(), P(), P("lat", "lon", None))
    return jax.shard_map(
        local,
        mesh=mesh,
        in_specs=placed,
        out_specs=(P("lat", "lon", None), P("lat", "lon", None), P()),
        check_vma=False,
    )
```

time: 435 us -> 53.3 us (0.12)
  waiting for transfers between devices: 239 us -> 0 us
  local copies, waits for them, and re-layouts: 91.8 us -> 7.61 us
  Pallas kernels: 0 us -> 43.5 us
  starting transfers between devices: 38.9 us -> 0 us
  matrix products: 32 us -> 0 us
  between operations: 14.5 us -> 0.71 us
  other arithmetic: 14.7 us -> 1.14 us
    psum x1 -> x0, waiting for transfers between devices: 235 us -> none  [local(): lax.psum(local_grad, ('lat', 'lon')) * (1.0 / math.sqrt(cell_count))]
    reshape x6 -> x1, local copies, waits for them, and re-layouts: 60.5 us -> 0.15 us  [local(): taps = taps.reshape(PAIRS, 2, BASES, 3 * SLOT)]
    pallas_call x0 -> x1, Pallas kernels: none -> 43.5 us  [local(): pl.pallas_call(functools.partial(kernel, n_lat, n_lon), out_shape=(jax.Sh...]
    ppermute x12 -> x0, starting transfers between devices: 38.8 us -> none  [the longest x6 20 us: with_halo(): lax.ppermute(lax.slice_in_dim(block, 0, width, axis=dim), axis, backward)]
    dot_general x14 -> x0, matrix products: 32 us -> none  [the longest x3 7.13 us: local(): jnp.einsum('kbxl,kbxc->klc', adjoint_blocks[start_row:start_row + row_cou...]
    mul x4 -> x0, local copies, waits for them, and re-layouts: 11.3 us -> none  [the longest x2 8.43 us: local(): gathered.reshape(row_count, col_count, group_count, group_width)]
    convert_element_type x5 -> x0, local copies, waits for them, and re-layouts: 11.2 us -> none  [the longest x2 9.73 us: local(): infilled = jnp.einsum('ibjgc,gbco->ijgo', scaled, mixing, preferred_eleme...]
    convert_element_type x3 -> x0, other arithmetic: 10.4 us -> none  [the longest x1 9.37 us: local(): scaled = (numerator.reshape(row_count, basis_count, col_count, group_coun...]
  transfers between devices with their start and end apart: 13 -> 0, of which waited for: 3 -> 0; matrix products, arithmetic and copies ran while one was open for 31% -> 0% of each run, Pallas kernels for 0% -> 0%
where the time goes in v1:
time: 53.3 us; the launch traced here: 52.9 us
  Pallas kernels  43.5 us (82%)
  local copies, waits for them, and re-layouts  7.61 us (14%)
  other arithmetic  1.14 us (2%)
  between operations  0.71 us (1%)
    pallas_call x1, Pallas kernels, local(): pl.pallas_call(functools.partial(kernel, n_lat, n_lon), out_shape=(jax.Sh...  43.5 us
    unnamed x13, local copies, waits for them, and re-layouts  4.62 us
    pallas_call x2, local copies, waits for them, and re-layouts, local(): pl.pallas_call(functools.partial(kernel, n_lat, n_lon), out_shape=(jax.Sh...  1.94 us

profile of v1, /device:TPU:1, one launch (start us, length us, event | category | flops | bytes accessed | tf_op | source)
XLA Modules:
  0.0 52.9 jit_solution(8245023591514759263)
XLA Ops:
  0.7 0.8 %dynamic_slice.6 = s32[24]{0:T(128)S(1)} dynamic-slice(s32[384]{0:T(512)} %param.9, s32[]{:T(128)S(6)} %select_n.8), dynamic_slice_sizes={24} | dynamic-slice | bytes 196 | tf_op jit(solution)/shard_map/dynamic_slice | solution.py:343
  1.4 0.1 broadcast_compare_fusion
  1.5 1.0 %convert_select_fusion = f32[24,4,3,17]{0,1,3,2:T(4,128)S(1)} fusion(bf16[384,4,3,17]{0,1,3,2:T(4,128)(2,1)} %param.8, s32[]{:T(128)S(6)} %select_n.8, pred[24,3,17]{0,2,1:T(8,128)(4,1)S(1)} %broadcast_and_fusion), kind=kLoop, calls=%fused_computation | loop fusion | flops 9792 | bytes 30604 | tf_op jit(solution)/shard_map/jit(_where)/select_n | solution.py:348
  2.5 0.2 copy.25
  2.8 0.0 copy-start.1
  2.8 0.1 reshape.75
  2.9 0.1 pad_bitcast_fusion
  3.1 0.7 %copy-done.1 = bf16[24,45,256]{2,0,1:T(8,128)(2,1)S(1)} copy-done((bf16[24,45,256]{2,0,1:T(8,128)(2,1)S(1)}, bf16[24,45,256]{2,0,1:T(8,128)(2,1)}, u32[]{:S(2)}) %copy-start.1) | copy-done | bytes 552984
  3.8 0.0 copy-start.3
  3.8 0.1 copy.19.feat
  3.9 0.8 %copy-done.3 = s32[24,45,8]{1,2,0:T(8,128)S(1)} copy-done((s32[24,45,8]{1,2,0:T(8,128)S(1)}, s32[24,45,8]{1,2,0:T(8,128)}, u32[]{:S(2)}) %copy-start.3) | copy-done | bytes 34584
  4.7 0.0 copy-start.2
  4.7 0.3 copy.20.mask
  5.0 0.8 %copy-done.2 = bf16[24,45,256]{2,0,1:T(8,128)(2,1)S(1)} copy-done((bf16[24,45,256]{2,0,1:T(8,128)(2,1)S(1)}, bf16[24,45,256]{2,0,1:T(8,128)(2,1)}, u32[]{:S(2)}) %copy-start.2) | copy-done | bytes 552984
  5.8 0.0 copy-start
  5.8 0.1 copy.21.cot
  5.9 0.8 %copy-done = bf16[8,4,32,32]{3,2,1,0:T(8,128)(2,1)S(1)} copy-done((bf16[8,4,32,32]{3,2,1,0:T(8,128)(2,1)S(1)}, bf16[8,4,32,32]{3,2,1,0:T(8,128)(2,1)}, u32[]{:S(2)}) %copy-start) | copy-done | bytes 65560
  6.7 43.5 %shard_map.85 = (bf16[24,45,256]{2,1,0:T(8,128)(2,1)S(1)}, bf16[24,45,256]{2,1,0:T(8,128)(2,1)S(1)}, f32[8,4,32,32]{3,2,1,0:T(8,128)S(1)}) custom-call(bf16[24,45,256]{2,1,0:T(8,128)(2,1)S(1)} %copy.19.feat, s32[24,45,8]{2,1,0:T(8,128)S(1)} %copy.20.mask, f32[24,4,256]{2,1,0:T(4,128)S(1)} %bitcast.11, bf16[8,4,32,32]{3,2,1,0:T(8,128)(2,1)S(1)} %copy-done, ...), custom_call_target="tpu_custom_call" | custom-call | tf_op jit(solution)/shard_map/pallas_call | solution.py:360
  50.2 1.0 %copy.22 = bf16[24,45,256]{2,0,1:T(8,128)(2,1)} copy(bf16[24,45,256]{2,1,0:T(8,128)(2,1)S(1)} %get-tuple-element.6) | data formatting | bytes 1105920 | tf_op jit(solution)/shard_map/pallas_call | solution.py:360
  51.2 1.0 %copy.23 = bf16[24,45,256]{2,0,1:T(8,128)(2,1)} copy(bf16[24,45,256]{2,1,0:T(8,128)(2,1)S(1)} %get-tuple-element.7) | data formatting | bytes 1105920 | tf_op jit(solution)/shard_map/pallas_call | solution.py:360
  52.1 0.8 %copy.27 = f32[8,4,32,32]{3,2,1,0:T(8,128)} copy(f32[8,4,32,32]{3,2,1,0:T(8,128)S(1)} %get-tuple-element.18) | data formatting | bytes 262144
  (8 shorter events, 0.1 us)
Async XLA Ops:
  2.8 1.1 %copy-start.1 = (bf16[24,45,256]{2,0,1:T(8,128)(2,1)S(1)}, bf16[24,45,256]{2,0,1:T(8,128)(2,1)}, u32[]{:S(2)}) copy-start(bf16[24,45,256]{2,0,1:T(8,128)(2,1)} %param.6) | copy-start | bytes 1658884
  3.8 0.9 %copy-start.3 = (s32[24,45,8]{1,2,0:T(8,128)S(1)}, s32[24,45,8]{1,2,0:T(8,128)}, u32[]{:S(2)}) copy-start(s32[24,45,8]{1,2,0:T(8,128)} %param.7) | copy-start | bytes 103684
  4.7 1.1 %copy-start.2 = (bf16[24,45,256]{2,0,1:T(8,128)(2,1)S(1)}, bf16[24,45,256]{2,0,1:T(8,128)(2,1)}, u32[]{:S(2)}) copy-start(bf16[24,45,256]{2,0,1:T(8,128)(2,1)} %param.11) | copy-start | bytes 1658884
  5.8 0.9 %copy-start = (bf16[8,4,32,32]{3,2,1,0:T(8,128)(2,1)S(1)}, bf16[8,4,32,32]{3,2,1,0:T(8,128)(2,1)}, u32[]{:S(2)}) copy-start(bf16[8,4,32,32]{3,2,1,0:T(8,128)(2,1)} %mix.1) | copy-start | bytes 196612

commit v2 on v1

v2 whole, which is shorter than its diff:
```python
import functools
import math

import jax
import jax.numpy as jnp
from jax import lax
from jax.experimental import pallas as pl
from jax.experimental.pallas import tpu as pltpu
from jax.sharding import PartitionSpec as P

MESH = pl.DeviceIdType.MESH
F32 = jnp.float32
BF16 = jnp.bfloat16
ROWS = 24
COLS = 45
PADC = 48
SLOT = 64
CHAN = 256
GROUPS = 8
WIDTH = 32
BASES = 4
REACH = 8
TAPS = 2 * REACH + 1
PAIRS = ROWS // 2
BAND = 2 * BASES * PADC


def far_first(sizes):
    steps = [(a, b) for a in range(sizes[0]) for b in range(sizes[1])]
    hops = lambda s: sum(min(k, n - k) for k, n in zip(s, sizes))
    return sorted(steps, key=lambda s: (-hops(s), s))[:-1]


PLANE = far_first((4, 4))
LINE = far_first((2, 8))


def iota(shape, dim):
    return lax.broadcasted_iota(jnp.int32, shape, dim)


def one_hot(test):
    return jnp.where(test, 1.0, 0.0).astype(BF16)


def dot(a, b):
    return jnp.dot(a, b, preferred_element_type=F32)


def pad_rows(x):
    return jnp.concatenate([x, jnp.zeros((PADC - COLS, x.shape[1]), F32)], axis=0)


def kernel(
    n_lat, n_lon,
    feat, mask, taps, width, mix, cot,
    infilled, input_grad, weight_sum,
    feat_own, mask_own, taps_own, mix_own, cot_own,
    wide_feat, wide_cot, tap_rows, base,
    field, seen, cots, cots_t, mixer, band, scaled, pulled, inverse, total,
    from_right, from_left, marks, marks_right, marks_left, marks_corner, mark_top, mark_bottom,
    corners, share, got_plane, got_line, final,
    part_right, part_left, part_top, part_bottom, part_corner,
    load_sem, store_sem, halo_send, halo_recv, part_send, part_recv, sum_send, sum_recv,
):
    la, lo = lax.axis_index("lat"), lax.axis_index("lon")
    up, down = lax.rem(la + n_lat - 1, n_lat), lax.rem(la + 1, n_lat)
    left, right = lax.rem(lo + n_lon - 1, n_lon), lax.rem(lo + 1, n_lon)

    loads = [
        pltpu.make_async_copy(src, dst, load_sem.at[n])
        for n, (src, dst) in enumerate(
            (
                (mask, mask_own), (feat, feat_own), (taps, taps_own),
                (cot, cot_own), (mix, mix_own),
            )
        )
    ]
    for copy in loads:
        copy.start()

    chip_y, core = la // 4, lax.rem(la, 2)
    chip_x, chip_z = 2 * lax.rem(la // 2, 2) + lo // 8, lax.rem(lo, 8)
    plane_rank, line_rank = 4 * chip_y + chip_x, 8 * core + chip_z

    def plane(step):
        y, x = lax.rem(chip_y + step[0], 4), lax.rem(chip_x + step[1], 4)
        return 4 * y + x, (4 * y + 2 * (x // 2) + core, 8 * lax.rem(x, 2) + chip_z)

    def line_of(step):
        other, z = lax.rem(core + step[0], 2), lax.rem(chip_z + step[1], 8)
        return 8 * other + z, (la - core + other, lo - chip_z + z)

    barrier = pltpu.get_barrier_semaphore()

    def greet(dev_lat, dev_lon):
        pl.semaphore_signal(
            barrier, inc=1, device_id=(dev_lat, dev_lon), device_id_type=MESH
        )

    for dev_lat in (up, down):
        for dev_lon in (left, right):
            greet(dev_lat, dev_lon)

    greet(la, left)
    greet(la, right)
    greet(up, lo)
    greet(down, lo)
    for step in PLANE:
        greet(*plane(step)[1])
    for step in LINE:
        greet(*line_of(step)[1])

    def remote(src, dst, send, recv, dev_lat, dev_lon):
        return pltpu.make_async_remote_copy(
            src_ref=src, dst_ref=dst, send_sem=send, recv_sem=recv,
            device_id=(dev_lat, dev_lon), device_id_type=MESH,
        )

    edge = pl.ds(0, PADC)
    head, tail = pl.ds(0, 16), pl.ds(32, 16)
    halo_plan = (
        (feat.at[pl.ds(0, REACH)], from_right, la, left),
        (feat.at[pl.ds(COLS - REACH, REACH)], from_left, la, right),
        (marks, marks_right, la, left),
        (marks, marks_left, la, right),
        (mask_own.at[0], mark_bottom, up, lo),
        (mask_own.at[ROWS - 1], mark_top, down, lo),
        (marks, marks_corner.at[0], up, left),
        (marks, marks_corner.at[1], up, right),
        (marks, marks_corner.at[2], down, left),
        (marks, marks_corner.at[3], down, right),
        (field.at[1, edge], field.at[ROWS + 1, edge], up, lo),
        (field.at[ROWS, edge], field.at[0, edge], down, lo),
        (field.at[1, head], corners.at[0], up, left),
        (field.at[1, tail], corners.at[1], up, right),
        (field.at[ROWS, head], corners.at[2], down, left),
        (field.at[ROWS, tail], corners.at[3], down, right),
    )
    halos = [
        remote(src, dst, halo_send.at[n], halo_recv.at[n], dev_lat, dev_lon)
        for n, (src, dst, dev_lat, dev_lon) in enumerate(halo_plan)
    ]

    pl.semaphore_wait(barrier, 8 + len(PLANE) + len(LINE))
    for copy in halos[0:2]:
        copy.start()

    loads[0].wait()
    flags = mask_own[...].reshape(ROWS * GROUPS, COLS).astype(F32).T.astype(BF16)
    row, col = iota((16, COLS), 0), iota((16, COLS), 1)
    pick = one_hot(col == jnp.where(row < 8, row, row + COLS - 16))
    marks[...] = dot(pick, flags).astype(BF16)
    for copy in halos[2:10]:
        copy.start()

    def widen(ref, n, rows):
        where = pl.ds(pl.multiple_of(ROWS * n, 8), ROWS)
        rows = rows.astype(F32)
        ref[0, where] = rows[:, 0:128]
        ref[1, where] = rows[:, 128:256]

    def cycle_of(ref, i, count):
        where = pl.ds(i, count, stride=ROWS)
        return jnp.concatenate([ref[0, where], ref[1, where]], axis=1)

    loads[1].wait()

    @pl.loop(0, COLS, unroll=5)
    def _(n):
        widen(wide_feat, n, feat_own[n])

    def spread(values, i):
        n, k = divmod(i, 16)
        part = values[:, 128 * n : min(128 * n + 128, ROWS * GROUPS)]
        depth = part.shape[1]
        table = one_hot(
            iota((depth, CHAN), 0) == iota((depth, CHAN), 1) // WIDTH + GROUPS * k
        )
        return dot(part, table)

    order = [0, ROWS - 1] + list(range(1, ROWS - 1))
    for i in order:
        wide = spread(flags, i)
        field[i + 1, 0:PADC] = pad_rows(
            cycle_of(wide_feat, i, COLS) * wide
        ).astype(BF16)
        seen[i + 1, 0:PADC] = pad_rows(wide).astype(BF16)
        if i == ROWS - 1:
            for copy in halos[10:]:
                copy.start()

    loads[2].wait()
    cycle = iota((BASES, n_lat * ROWS), 1)
    for a in range(3):
        outside = {0: cycle == 0, 1: cycle < 0, 2: cycle == n_lat * ROWS - 1}[a]
        for e in range(TAPS):
            first = BASES * (TAPS * a + e)
            tap_rows[first : first + BASES] = jnp.where(
                outside, 0.0, taps_own[a, e].astype(F32)
            )
    tap_rows[BASES * 3 * TAPS :] = jnp.zeros((8 - BASES * 3 * TAPS % 8, n_lat * ROWS), F32)
    shape = (ROWS, n_lat * ROWS)
    choose = one_hot(iota(shape, 1) == iota(shape, 0) + la * ROWS)
    mine = lax.dot_general(
        choose, tap_rows[...].astype(BF16), (((1,), (1,)), ((), ())), preferred_element_type=F32
    ).astype(BF16)
    shape = (mine.shape[1], CHAN)
    slot, entry = iota(shape, 1) // SLOT, iota(shape, 1) % SLOT
    odd = iota((ROWS, CHAN), 0) % 2 == 1
    away = jnp.abs(iota((1, CHAN), 1) % SLOT - REACH)
    for b in range(BASES):
        home = (entry < TAPS) & (slot < 3) & (
            iota(shape, 0) == BASES * (TAPS * slot + entry) + b
        )
        line = dot(mine, one_hot(home))
        line = jnp.where(odd, pltpu.roll(line, SLOT, 1), line)
        for i in range(ROWS):
            base[i, b : b + 1] = jnp.where(
                away <= width[la * ROWS + i], line[i : i + 1], 0.0
            )

    lane = iota((PADC, 128), 1) % SLOT

    @pl.loop(0, PAIRS, unroll=2)
    def _(t):
        for k in range(2):
            for b in range(BASES):
                for v in range(2):
                    line = base[2 * t + k, b : b + 1, v * 128 : v * 128 + 128]
                    row = jnp.broadcast_to(line, (PADC, 128))
                    late = pltpu.roll(jnp.broadcast_to(line, (8, 128)), 3, 1)
                    late = jnp.concatenate([late, late], axis=0)
                    own = pltpu.roll(row, 120, 1, stride=1, stride_axis=0)
                    high = pltpu.roll(late, 24, 1, stride=1, stride_axis=0)
                    low = pltpu.roll(row[0:8], 56, 1, stride=1, stride_axis=0)
                    piece = jnp.concatenate(
                        [
                            jnp.where(
                                lane[0:8] < COLS, own[0:8], jnp.where(lane[0:8] < 56, 0.0, low)
                            ),
                            own[8:32],
                            jnp.where(
                                lane[0:16] < COLS,
                                own[32:48],
                                jnp.where(
                                    (lane[0:16] >= PADC) & (lane[0:16] < 56), high, 0.0
                                ),
                            ),
                        ],
                        axis=0,
                    )
                    start = (k * BASES + b) * PADC
                    band[t, start : start + PADC, v * 128 : v * 128 + 128] = piece.astype(BF16)

    loads[3].wait()

    @pl.loop(0, COLS, unroll=5)
    def _(n):
        widen(wide_cot, n, cot_own[n])

    for i in range(ROWS):
        cots[i * PADC : i * PADC + PADC] = pad_rows(
            cycle_of(wide_cot, i, COLS)
        ).astype(BF16)
    for n in range(ROWS * PADC // 128):
        cots_t[:, n * 128 : n * 128 + 128] = cots[n * 128 : n * 128 + 128].T

    for copy in halos[2:]:
        copy.wait_recv()
    upper = iota((16, ROWS * GROUPS), 0) < 8

    def merged(high, low):
        return jnp.where(upper, high.astype(F32), low.astype(F32)).astype(BF16)

    both = merged(marks_right[...], marks_left[...])
    one_row = one_hot(iota((GROUPS, CHAN), 1) // WIDTH == iota((GROUPS, CHAN), 0))
    for i, ref, cycle, high, low in (
        (0, mark_top, ROWS - 1, 2, 3), (ROWS + 1, mark_bottom, 0, 0, 1)
    ):
        flat = dot(ref[...].astype(F32).T.astype(BF16), one_row)
        seen[i, 0:PADC] = pad_rows(flat).astype(BF16)
        pair = merged(marks_corner[high], marks_corner[low])
        seen[i, PADC:SLOT] = spread(pair, cycle).astype(BF16)
        ends = pltpu.roll(corners[low].astype(F32), 11, 0)
        field[i, PADC:SLOT] = jnp.concatenate(
            [corners[high].astype(F32)[0:8], ends[0:8]], axis=0
        ).astype(BF16)
    for copy in halos[0:2]:
        copy.wait_recv()

    @pl.loop(0, REACH, unroll=4)
    def _(n):
        widen(wide_feat, n, from_right[n])
        widen(wide_feat, n + REACH, from_left[n])

    for i in range(ROWS):
        wide = spread(both, i)
        field[i + 1, PADC:SLOT] = (
            cycle_of(wide_feat, i, 2 * REACH) * wide
        ).astype(BF16)
        seen[i + 1, PADC:SLOT] = wide.astype(BF16)

    @pl.loop(0, PAIRS, unroll=2)
    def _(t):
        weights = band[t]
        numerator = dot(weights, field[pl.ds(2 * t, 4)].reshape(4 * SLOT, CHAN))
        denominator = dot(weights, seen[pl.ds(2 * t, 4)].reshape(4 * SLOT, CHAN))
        shrink = 1.0 / jnp.maximum(denominator, 1.0)
        normal = (numerator * shrink).astype(BF16)
        for k in range(2):
            start = pl.multiple_of((2 * t + k) * PADC, PADC)
            for b in range(BASES):
                first = (k * BASES + b) * PADC
                scaled[b, pl.ds(start, PADC)] = normal[first : first + PADC]
        inverse[t] = shrink

    block = iota((CHAN, CHAN), 0) // WIDTH == iota((CHAN, CHAN), 1) // WIDTH
    for b in range(BASES):
        grad = jnp.where(block, dot(cots_t[...], scaled[b]), 0.0)
        share[b * WIDTH : b * WIDTH + WIDTH] = jnp.sum(grad.reshape(GROUPS, WIDTH, CHAN), axis=0)

    def gather_share(n):
        to, device = plane(PLANE[n])
        rows = pl.ds(pl.multiple_of(to * 8, 8), 8)
        return remote(
            share.at[rows], got_plane.at[n], sum_send.at[0, n], sum_recv.at[0, n], *device
        )

    def swap_share(n):
        _, device = line_of(LINE[n])
        here = got_line.at[line_rank]
        return remote(here, here, sum_send.at[1, n], sum_recv.at[1, n], *device)

    def spread_share(n):
        _, device = plane(PLANE[n])
        here = final.at[plane_rank]
        return remote(here, here, sum_send.at[2, n], sum_recv.at[2, n], *device)

    def start_all(make):
        copies = [make(n) for n in range(15)]
        for copy in copies:
            copy.start()
        return copies

    def finish_all(copies):
        for copy in copies:
            copy.wait_recv()

    gathers = start_all(gather_share)

    loads[4].wait()
    repeat = one_hot(iota((WIDTH, CHAN), 1) % WIDTH == iota((WIDTH, CHAN), 0))
    for b in range(BASES):
        tall = mix_own[:, b].reshape(CHAN, WIDTH)
        mixer[b] = jnp.where(block, dot(tall, repeat), 0.0).astype(BF16)

    @pl.loop(0, PAIRS // 4)
    def _(n):
        start = pl.multiple_of(n * 8 * PADC, 8 * PADC)
        rows = cots[pl.ds(start, 8 * PADC)]
        for b in range(BASES):
            result = lax.dot_general(
                rows, mixer[b], (((1,), (1,)), ((), ())), preferred_element_type=F32
            )
            for i in range(8):
                first = ((i % 2) * BASES + b) * PADC
                here = 4 * n + i // 2
                pulled[here, first : first + PADC] = (
                    result[i * PADC : i * PADC + PADC] * inverse[here, first : first + PADC]
                ).astype(BF16)

    total[0:2] = jnp.zeros((2, SLOT, CHAN), F32)

    @pl.loop(0, PAIRS, unroll=2)
    def _(t):
        result = dot(band[t].T, pulled[t]).reshape(4, SLOT, CHAN)
        total[pl.ds(2 * t, 2)] += result[0:2]
        total[pl.ds(2 * t + 2, 2)] = result[2:4]

    inner = pl.ds(1, ROWS)
    high, low, own = pl.ds(PADC, 8), pl.ds(56, 8), pl.ds(0, PADC)
    part_plan = (
        (total.at[inner, low], part_right, la, left),
        (total.at[inner, high], part_left, la, right),
        (total.at[0, own], part_bottom, up, lo),
        (total.at[ROWS + 1, own], part_top, down, lo),
        (total.at[0, low], part_corner.at[0], up, left),
        (total.at[0, high], part_corner.at[1], up, right),
        (total.at[ROWS + 1, low], part_corner.at[2], down, left),
        (total.at[ROWS + 1, high], part_corner.at[3], down, right),
    )
    parts = [
        remote(src, dst, part_send.at[n], part_recv.at[n], dev_lat, dev_lon)
        for n, (src, dst, dev_lat, dev_lon) in enumerate(part_plan)
    ]
    for copy in parts:
        copy.start()

    finish_all(gathers)
    got_line[line_rank] = share[pl.ds(pl.multiple_of(plane_rank * 8, 8), 8)] + jnp.sum(
        got_plane[...], axis=0
    )
    swaps = start_all(swap_share)

    def spill(ref, i, rows):
        where = pl.ds(i, COLS, stride=ROWS)
        ref[0, where] = rows[0:COLS, 0:128]
        ref[1, where] = rows[0:COLS, 128:256]

    def narrow(ref, out):
        @pl.loop(0, COLS, unroll=5)
        def _(n):
            where = pl.ds(pl.multiple_of(ROWS * n, 8), ROWS)
            out[n] = jnp.concatenate([ref[0, where], ref[1, where]], axis=1).astype(BF16)

    @pl.loop(0, PAIRS // 4)
    def _(n):
        start = pl.multiple_of(n * 8 * PADC, 8 * PADC)
        result = dot(scaled[0, pl.ds(start, 8 * PADC)], mixer[0])
        for b in range(1, BASES):
            result += dot(scaled[b, pl.ds(start, 8 * PADC)], mixer[b])
        for i in range(8):
            spill(wide_cot, 8 * n + i, result[i * PADC : i * PADC + PADC])

    narrow(wide_cot, cot_own)
    stores = [pltpu.make_async_copy(cot_own, infilled, store_sem.at[0])]
    stores[0].start()

    finish_all(swaps)
    final[plane_rank] = jnp.sum(got_line[...], axis=0) * (
        1.0 / math.sqrt(ROWS * n_lat * COLS * n_lon)
    )
    spreads = start_all(spread_share)

    for copy in parts:
        copy.wait_recv()
    for copy in parts:
        copy.wait_send()

    part_left[0] += part_corner[3]
    part_right[0] += part_corner[2]
    part_left[ROWS - 1] += part_corner[1]
    part_right[ROWS - 1] += part_corner[0]
    total[1, 0:PADC] += part_top[...]
    total[ROWS, 0:PADC] += part_bottom[...]

    @pl.loop(0, ROWS, unroll=2)
    def _(i):
        after = pltpu.roll(
            jnp.concatenate([part_right[i], jnp.zeros((8, CHAN), F32)], axis=0), 5, 0
        )
        extra = jnp.concatenate([part_left[i], jnp.zeros((24, CHAN), F32), after], axis=0)
        result = (total[i + 1, 0:PADC] + extra) * seen[i + 1, 0:PADC].astype(F32)
        spill(wide_feat, i, result)

    narrow(wide_feat, feat_own)
    stores.append(pltpu.make_async_copy(feat_own, input_grad, store_sem.at[1]))
    stores[1].start()
    for copy in halos:
        copy.wait_send()

    for copy in gathers + swaps:
        copy.wait_send()

    finish_all(spreads)
    for copy in spreads:
        copy.wait_send()
    stores.append(pltpu.make_async_copy(final, weight_sum, store_sem.at[2]))
    stores[2].start()
    for copy in stores:
        copy.wait()


def finish(
    sums, first, second, grads, first_out, second_out, held, sums_own, grads_own, in_sem, out_sem
):
    load_sums = pltpu.make_async_copy(sums, sums_own, in_sem.at[6])
    load_sums.start()
    step = COLS // 3
    loads, stores = [], []
    for n, (src, dst) in enumerate(((first, first_out), (second, second_out))):
        for k in range(3):
            part = pl.ds(k * step, step)
            loads.append(
                pltpu.make_async_copy(src.at[part], held.at[n, part], in_sem.at[3 * n + k])
            )
            stores.append(
                pltpu.make_async_copy(held.at[n, part], dst.at[part], out_sem.at[3 * n + k])
            )
    for copy in loads:
        copy.start()
    load_sums.wait()
    for b in range(BASES):
        grad = sums_own[4 * b : 4 * b + 4].reshape(WIDTH, CHAN)
        grads_own[:, b] = grad.T.reshape(GROUPS, WIDTH, WIDTH)
    stores.append(pltpu.make_async_copy(grads_own, grads, out_sem.at[6]))
    stores[6].start()
    for load, store in zip(loads, stores):
        load.wait()
        store.start()
    for copy in stores:
        copy.wait()


def local(features, obs_mask, filter_taps, band_width, mixing, cotangent):
    n_lat, n_lon = lax.axis_size("lat"), lax.axis_size("lon")
    anywhere = pl.BlockSpec(memory_space=pltpu.HBM)
    marks = pltpu.VMEM((16, ROWS * GROUPS), BF16)
    field = jax.ShapeDtypeStruct((COLS, ROWS, CHAN), BF16)
    infilled, input_grad, sums = pl.pallas_call(
        functools.partial(kernel, n_lat, n_lon),
        out_shape=(
            field,
            field,
            jax.ShapeDtypeStruct((n_lon, 8, CHAN), F32),
        ),
        in_specs=[anywhere] * 3 + [pl.BlockSpec(memory_space=pltpu.SMEM)] + [anywhere] * 2,
        out_specs=(anywhere,) * 3,
        scratch_shapes=[
            pltpu.VMEM((COLS, ROWS, CHAN), BF16),
            pltpu.VMEM((ROWS, GROUPS, COLS), jnp.int32),
            pltpu.VMEM((3, TAPS, BASES, n_lat * ROWS), BF16),
            pltpu.VMEM((GROUPS, BASES, WIDTH, WIDTH), BF16),
            pltpu.VMEM((COLS, ROWS, CHAN), BF16),
            pltpu.VMEM((2, COLS * ROWS, 128), F32),
            pltpu.VMEM((2, COLS * ROWS, 128), F32),
            pltpu.VMEM((208, n_lat * ROWS), F32),
            pltpu.VMEM((ROWS, BASES, CHAN), F32),
            pltpu.VMEM((ROWS + 2, SLOT, CHAN), BF16),
            pltpu.VMEM((ROWS + 2, SLOT, CHAN), BF16),
            pltpu.VMEM((ROWS * PADC, CHAN), BF16),
            pltpu.VMEM((CHAN, ROWS * PADC), BF16),
            pltpu.VMEM((BASES, CHAN, CHAN), BF16),
            pltpu.VMEM((PAIRS, BAND, 4 * SLOT), BF16),
            pltpu.VMEM((BASES, ROWS * PADC, CHAN), BF16),
            pltpu.VMEM((PAIRS, BAND, CHAN), BF16),
            pltpu.VMEM((PAIRS, BAND, CHAN), F32),
            pltpu.VMEM((ROWS + 2, SLOT, CHAN), F32),
            pltpu.VMEM((REACH, ROWS, CHAN), BF16),
            pltpu.VMEM((REACH, ROWS, CHAN), BF16),
            marks, marks, marks,
            pltpu.VMEM((4, 16, ROWS * GROUPS), BF16),
            pltpu.VMEM((GROUPS, COLS), jnp.int32),
            pltpu.VMEM((GROUPS, COLS), jnp.int32),
            pltpu.VMEM((4, 16, CHAN), BF16),
            pltpu.VMEM((BASES * WIDTH, CHAN), F32),
            pltpu.VMEM((15, 8, CHAN), F32),
            pltpu.VMEM((16, 8, CHAN), F32),
            pltpu.VMEM((16, 8, CHAN), F32),
            pltpu.VMEM((ROWS, 8, CHAN), F32),
            pltpu.VMEM((ROWS, 8, CHAN), F32),
            pltpu.VMEM((PADC, CHAN), F32),
            pltpu.VMEM((PADC, CHAN), F32),
            pltpu.VMEM((4, 8, CHAN), F32),
            pltpu.SemaphoreType.DMA((5,)),
            pltpu.SemaphoreType.DMA((3,)),
            pltpu.SemaphoreType.DMA((16,)),
            pltpu.SemaphoreType.DMA((16,)),
            pltpu.SemaphoreType.DMA((8,)),
            pltpu.SemaphoreType.DMA((8,)),
            pltpu.SemaphoreType.DMA((3, 16)),
            pltpu.SemaphoreType.DMA((3, 16)),
        ],
        compiler_params=pltpu.CompilerParams(
            collective_id=0, has_side_effects=True, vmem_limit_bytes=56 * 1024 * 1024
        ),
    )(
        features.transpose(1, 0, 2),
        obs_mask.transpose(0, 2, 1),
        filter_taps.transpose(2, 3, 1, 0),
        band_width,
        mixing,
        cotangent.transpose(1, 0, 2),
    )
    weight_grad, infilled, input_grad = pl.pallas_call(
        finish,
        out_shape=(jax.ShapeDtypeStruct((GROUPS, BASES, WIDTH, WIDTH), F32), field, field),
        in_specs=[anywhere] * 3,
        out_specs=(anywhere,) * 3,
        scratch_shapes=[
            pltpu.VMEM((2, COLS, ROWS, CHAN), BF16),
            pltpu.VMEM((n_lon, 8, CHAN), F32),
            pltpu.VMEM((GROUPS, BASES, WIDTH, WIDTH), F32),
            pltpu.SemaphoreType.DMA((7,)),
            pltpu.SemaphoreType.DMA((7,)),
        ],
        compiler_params=pltpu.CompilerParams(vmem_limit_bytes=56 * 1024 * 1024),
    )(sums, infilled, input_grad)
    return infilled.transpose(1, 0, 2), input_grad.transpose(1, 0, 2), weight_grad


def solution(mesh):
    placed = (P("lat", "lon", None), P("lat", "lon", None), P(), P(), P(), P("lat", "lon", None))
    return jax.shard_map(
        local,
        mesh=mesh,
        in_specs=placed,
        out_specs=(P("lat", "lon", None), P("lat", "lon", None), P()),
        check_vma=False,
    )
```

time: 53.3 us -> 45.1 us (0.85)
  local copies, waits for them, and re-layouts: 7.61 us -> 0 us
  other arithmetic: 1.14 us -> 0 us
  Pallas kernels: 43.5 us -> 44.4 us
    unnamed x13 -> x0, local copies, waits for them, and re-layouts: 4.62 us -> none
    pallas_call x2 -> x0, local copies, waits for them, and re-layouts: 1.94 us -> none  [local(): pl.pallas_call(functools.partial(kernel, n_lat, n_lon), out_shape=(jax.Sh...]
    select_n x1 -> x0, other arithmetic: 1.01 us -> none  [local(): taps = jnp.where(keep, taps, 0.0)]
    pallas_call x1 -> x2, Pallas kernels: 43.5 us -> 44.4 us  [the longest x1 42 us: local(): pl.pallas_call(functools.partial(kernel, n_lat, n_lon), out_shape=(field,...]
    dynamic_slice x1 -> x0, local copies, waits for them, and re-layouts: 0.76 us -> none  [local(): width = lax.dynamic_slice_in_dim(band_width, first, ROWS, 0)]
where the time goes in v2:
time: 45.1 us; the launch traced here: 45 us
  Pallas kernels  44.4 us (98%)
  between operations  0.64 us (1%)
    pallas_call x1, Pallas kernels, local(): pl.pallas_call(functools.partial(kernel, n_lat, n_lon), out_shape=(field,...  42 us
    pallas_call x1, Pallas kernels, local(): pl.pallas_call(finish, out_shape=(jax.ShapeDtypeStruct((GROUPS, BASES, WI...  2.38 us

profile of v2, /device:TPU:1, one launch (start us, length us, event | category | flops | bytes accessed | tf_op | source)
XLA Modules:
  0.0 45.0 jit_solution(3640410359361102624)
XLA Ops:
  0.6 42.0 %shard_map.85 = (bf16[45,24,256]{2,1,0:T(8,128)(2,1)}, bf16[45,24,256]{2,1,0:T(8,128)(2,1)}, f32[16,8,256]{2,1,0:T(8,128)}) custom-call(bf16[45,24,256]{2,1,0:T(8,128)(2,1)} %bitcast.6, s32[24,8,45]{2,1,0:T(8,128)} %bitcast.9, bf16[3,17,4,384]{3,2,1,0:T(4,128)(2,1)} %bitcast.8, s32[384]{0:T(512)} %width.1, bf16[8,4,32,32]{3,2,1,0:T(8,128)(2,1)} %mix.1, ...), custom_call_target="tpu_custom_call" | custom-call | tf_op jit(solution)/shard_map/pallas_call | solution.py:511
  42.6 2.4 %shard_map.86 = (f32[8,4,32,32]{3,2,1,0:T(8,128)}, bf16[45,24,256]{2,1,0:T(8,128)(2,1)}, bf16[45,24,256]{2,1,0:T(8,128)(2,1)}) custom-call(f32[16,8,256]{2,1,0:T(8,128)} %get-tuple-element.9.sums, bf16[45,24,256]{2,1,0:T(8,128)(2,1)} %get-tuple-element.10.first, bf16[45,24,256]{2,1,0:T(8,128)(2,1)} %get-tuple-element.11.second), custom_call_target="tpu_custom_call" | custom-call | tf_op jit(solution)/shard_map/pallas_call | solution.py:576

commit v3 on v2

--- a/solution.py
+++ b/solution.py
@@ -57,7 +57,7 @@
     infilled, input_grad, weight_sum,
     feat_own, mask_own, taps_own, mix_own, cot_own,
     wide_feat, wide_cot, tap_rows, base,
-    field, seen, cots, cots_t, mixer, band, scaled, pulled, inverse, total,
+    field, seen, cots, cots_t, mixer, band, scaled, pulled, back, total,
     from_right, from_left, marks, marks_right, marks_left, marks_corner, mark_top, mark_bottom,
     corners, share, got_plane, got_line, final,
     part_right, part_left, part_top, part_bottom, part_corner,
@@ -222,7 +222,7 @@
 
     lane = iota((PADC, 128), 1) % SLOT
 
-    @pl.loop(0, PAIRS, unroll=2)
+    @pl.loop(0, PAIRS)
     def _(t):
         for k in range(2):
             for b in range(BASES):
@@ -266,6 +266,25 @@
     for n in range(ROWS * PADC // 128):
         cots_t[:, n * 128 : n * 128 + 128] = cots[n * 128 : n * 128 + 128].T
 
+    loads[4].wait()
+    block = iota((CHAN, CHAN), 0) // WIDTH == iota((CHAN, CHAN), 1) // WIDTH
+    repeat = one_hot(iota((WIDTH, CHAN), 1) % WIDTH == iota((WIDTH, CHAN), 0))
+    for b in range(BASES):
+        tall = mix_own[:, b].reshape(CHAN, WIDTH)
+        mixer[b] = jnp.where(block, dot(tall, repeat), 0.0).astype(BF16)
+
+    @pl.loop(0, PAIRS // 4)
+    def _(n):
+        start = pl.multiple_of(n * 8 * PADC, 8 * PADC)
+        rows = cots[pl.ds(start, 8 * PADC)]
+        for b in range(BASES):
+            result = lax.dot_general(
+                rows, mixer[b], (((1,), (1,)), ((), ())), preferred_element_type=F32
+            )
+            for i in range(8):
+                first = ((i % 2) * BASES + b) * PADC
+                back[4 * n + i // 2, first : first + PADC] = result[i * PADC : i * PADC + PADC]
+
     for copy in halos[2:]:
         copy.wait_recv()
     upper = iota((16, ROWS * GROUPS), 0) < 8
@@ -301,7 +320,7 @@
         ).astype(BF16)
         seen[i + 1, PADC:SLOT] = wide.astype(BF16)
 
-    @pl.loop(0, PAIRS, unroll=2)
+    @pl.loop(0, PAIRS, unroll=4)
     def _(t):
         weights = band[t]
         numerator = dot(weights, field[pl.ds(2 * t, 4)].reshape(4 * SLOT, CHAN))
@@ -313,9 +332,8 @@
             for b in range(BASES):
                 first = (k * BASES + b) * PADC
                 scaled[b, pl.ds(start, PADC)] = normal[first : first + PADC]
-        inverse[t] = shrink
-
-    block = iota((CHAN, CHAN), 0) // WIDTH == iota((CHAN, CHAN), 1) // WIDTH
+        pulled[t] = (back[t] * shrink).astype(BF16)
+
     for b in range(BASES):
         grad = jnp.where(block, dot(cots_t[...], scaled[b]), 0.0)
         share[b * WIDTH : b * WIDTH + WIDTH] = jnp.sum(grad.reshape(GROUPS, WIDTH, CHAN), axis=0)
@@ -334,8 +352,9 @@
 
     def spread_share(n):
         _, device = plane(PLANE[n])
-        here = final.at[plane_rank]
-        return remote(here, here, sum_send.at[2, n], sum_recv.at[2, n], *device)
+        return remote(
+            final, weight_sum.at[plane_rank], sum_send.at[2, n], sum_recv.at[2, n], *device
+        )
 
     def start_all(make):
         copies = [make(n) for n in range(15)]
@@ -349,30 +368,9 @@
 
     gathers = start_all(gather_share)
 
-    loads[4].wait()
-    repeat = one_hot(iota((WIDTH, CHAN), 1) % WIDTH == iota((WIDTH, CHAN), 0))
-    for b in range(BASES):
-        tall = mix_own[:, b].reshape(CHAN, WIDTH)
-        mixer[b] = jnp.where(block, dot(tall, repeat), 0.0).astype(BF16)
-
-    @pl.loop(0, PAIRS // 4)
-    def _(n):
-        start = pl.multiple_of(n * 8 * PADC, 8 * PADC)
-        rows = cots[pl.ds(start, 8 * PADC)]
-        for b in range(BASES):
-            result = lax.dot_general(
-                rows, mixer[b], (((1,), (1,)), ((), ())), preferred_element_type=F32
-            )
-            for i in range(8):
-                first = ((i % 2) * BASES + b) * PADC
-                here = 4 * n + i // 2
-                pulled[here, first : first + PADC] = (
-                    result[i * PADC : i * PADC + PADC] * inverse[here, first : first + PADC]
-                ).astype(BF16)
-
     total[0:2] = jnp.zeros((2, SLOT, CHAN), F32)
 
-    @pl.loop(0, PAIRS, unroll=2)
+    @pl.loop(0, PAIRS, unroll=4)
     def _(t):
         result = dot(band[t].T, pulled[t]).reshape(4, SLOT, CHAN)
         total[pl.ds(2 * t, 2)] += result[0:2]
@@ -428,10 +426,12 @@
     stores[0].start()
 
     finish_all(swaps)
-    final[plane_rank] = jnp.sum(got_line[...], axis=0) * (
+    final[...] = jnp.sum(got_line[...], axis=0) * (
         1.0 / math.sqrt(ROWS * n_lat * COLS * n_lon)
     )
     spreads = start_all(spread_share)
+    stores.append(pltpu.make_async_copy(final, weight_sum.at[plane_rank], store_sem.at[2]))
+    stores[1].start()
 
     for copy in parts:
         copy.wait_recv()
@@ -456,7 +456,7 @@
 
     narrow(wide_feat, feat_own)
     stores.append(pltpu.make_async_copy(feat_own, input_grad, store_sem.at[1]))
-    stores[1].start()
+    stores[2].start()
     for copy in halos:
         copy.wait_send()
 
@@ -466,8 +466,6 @@
     finish_all(spreads)
     for copy in spreads:
         copy.wait_send()
-    stores.append(pltpu.make_async_copy(final, weight_sum, store_sem.at[2]))
-    stores[2].start()
     for copy in stores:
         copy.wait()
 
@@ -547,7 +545,7 @@
             pltpu.VMEM((BASES * WIDTH, CHAN), F32),
             pltpu.VMEM((15, 8, CHAN), F32),
             pltpu.VMEM((16, 8, CHAN), F32),
-            pltpu.VMEM((16, 8, CHAN), F32),
+            pltpu.VMEM((8, CHAN), F32),
             pltpu.VMEM((ROWS, 8, CHAN), F32),
             pltpu.VMEM((ROWS, 8, CHAN), F32),
             pltpu.VMEM((PADC, CHAN), F32),

time: 45.1 us -> 42.1 us (0.933)
  Pallas kernels: 44.4 us -> 41.4 us
    pallas_call x1, Pallas kernels: 42 us -> 39 us  [local(): pl.pallas_call(functools.partial(kernel, n_lat, n_lon), out_shape=(field,...]
where the time goes in v3:
time: 42.1 us; the launch traced here: 42 us
  Pallas kernels  41.4 us (98%)
  between operations  0.64 us (2%)
    pallas_call x1, Pallas kernels, local(): pl.pallas_call(functools.partial(kernel, n_lat, n_lon), out_shape=(field,...  39 us
    pallas_call x1, Pallas kernels, local(): pl.pallas_call(finish, out_shape=(jax.ShapeDtypeStruct((GROUPS, BASES, WI...  2.38 us

profile of v3, /device:TPU:1, one launch (start us, length us, event | category | flops | bytes accessed | tf_op | source)
XLA Modules:
  0.0 42.0 jit_solution(8989901668838376485)
XLA Ops:
  0.6 39.0 %shard_map.85 = (bf16[45,24,256]{2,1,0:T(8,128)(2,1)}, bf16[45,24,256]{2,1,0:T(8,128)(2,1)}, f32[16,8,256]{2,1,0:T(8,128)}) custom-call(bf16[45,24,256]{2,1,0:T(8,128)(2,1)} %bitcast.6, s32[24,8,45]{2,1,0:T(8,128)} %bitcast.9, bf16[3,17,4,384]{3,2,1,0:T(4,128)(2,1)} %bitcast.8, s32[384]{0:T(512)} %width.1, bf16[8,4,32,32]{3,2,1,0:T(8,128)(2,1)} %mix.1, ...), custom_call_target="tpu_custom_call" | custom-call | tf_op jit(solution)/shard_map/pallas_call | solution.py:509
  39.6 2.4 %shard_map.86 = (f32[8,4,32,32]{3,2,1,0:T(8,128)}, bf16[45,24,256]{2,1,0:T(8,128)(2,1)}, bf16[45,24,256]{2,1,0:T(8,128)(2,1)}) custom-call(f32[16,8,256]{2,1,0:T(8,128)} %get-tuple-element.9.sums, bf16[45,24,256]{2,1,0:T(8,128)(2,1)} %get-tuple-element.10.first, bf16[45,24,256]{2,1,0:T(8,128)(2,1)} %get-tuple-element.11.second), custom_call_target="tpu_custom_call" | custom-call | tf_op jit(solution)/shard_map/pallas_call | solution.py:574

commit v4 on v3

--- a/solution.py
+++ b/solution.py
@@ -60,7 +60,7 @@
     field, seen, cots, cots_t, mixer, band, scaled, pulled, back, total,
     from_right, from_left, marks, marks_right, marks_left, marks_corner, mark_top, mark_bottom,
     corners, share, got_plane, got_line, final,
-    part_right, part_left, part_top, part_bottom, part_corner,
+    send_low, send_high, part_right, part_left, part_top, part_bottom, part_corner,
     load_sem, store_sem, halo_send, halo_recv, part_send, part_recv, sum_send, sum_recv,
 ):
     la, lo = lax.axis_index("lat"), lax.axis_index("lon")
@@ -71,7 +71,7 @@
         pltpu.make_async_copy(src, dst, load_sem.at[n])
         for n, (src, dst) in enumerate(
             (
-                (mask, mask_own), (feat, feat_own), (taps, taps_own),
+                (feat, feat_own), (mask, mask_own), (taps, taps_own),
                 (cot, cot_own), (mix, mix_own),
             )
         )
@@ -79,13 +79,13 @@
     for copy in loads:
         copy.start()
 
-    chip_y, core = la // 4, lax.rem(la, 2)
-    chip_x, chip_z = 2 * lax.rem(la // 2, 2) + lo // 8, lax.rem(lo, 8)
+    chip_y, core = lax.div(la, 4), lax.rem(la, 2)
+    chip_x, chip_z = 2 * lax.rem(lax.div(la, 2), 2) + lax.div(lo, 8), lax.rem(lo, 8)
     plane_rank, line_rank = 4 * chip_y + chip_x, 8 * core + chip_z
 
     def plane(step):
         y, x = lax.rem(chip_y + step[0], 4), lax.rem(chip_x + step[1], 4)
-        return 4 * y + x, (4 * y + 2 * (x // 2) + core, 8 * lax.rem(x, 2) + chip_z)
+        return 4 * y + x, (4 * y + 2 * lax.div(x, 2) + core, 8 * lax.rem(x, 2) + chip_z)
 
     def line_of(step):
         other, z = lax.rem(core + step[0], 2), lax.rem(chip_z + step[1], 8)
@@ -120,8 +120,8 @@
     edge = pl.ds(0, PADC)
     head, tail = pl.ds(0, 16), pl.ds(32, 16)
     halo_plan = (
-        (feat.at[pl.ds(0, REACH)], from_right, la, left),
-        (feat.at[pl.ds(COLS - REACH, REACH)], from_left, la, right),
+        (feat_own.at[pl.ds(0, REACH)], from_right, la, left),
+        (feat_own.at[pl.ds(COLS - REACH, REACH)], from_left, la, right),
         (marks, marks_right, la, left),
         (marks, marks_left, la, right),
         (mask_own.at[0], mark_bottom, up, lo),
@@ -142,11 +142,12 @@
         for n, (src, dst, dev_lat, dev_lon) in enumerate(halo_plan)
     ]
 
+    loads[0].wait()
     pl.semaphore_wait(barrier, 8 + len(PLANE) + len(LINE))
     for copy in halos[0:2]:
         copy.start()
 
-    loads[0].wait()
+    loads[1].wait()
     flags = mask_own[...].reshape(ROWS * GROUPS, COLS).astype(F32).T.astype(BF16)
     row, col = iota((16, COLS), 0), iota((16, COLS), 1)
     pick = one_hot(col == jnp.where(row < 8, row, row + COLS - 16))
@@ -164,7 +165,6 @@
         where = pl.ds(i, count, stride=ROWS)
         return jnp.concatenate([ref[0, where], ref[1, where]], axis=1)
 
-    loads[1].wait()
 
     @pl.loop(0, COLS, unroll=5)
     def _(n):
@@ -376,11 +376,17 @@
         total[pl.ds(2 * t, 2)] += result[0:2]
         total[pl.ds(2 * t + 2, 2)] = result[2:4]
 
-    inner = pl.ds(1, ROWS)
+    @pl.loop(0, PAIRS, unroll=4)
+    def _(t):
+        for ref, first in ((send_high, PADC), (send_low, PADC + 8)):
+            ref[t] = jnp.concatenate(
+                [total[2 * t + k, first : first + 8] for k in (1, 2)], axis=0
+            ).astype(BF16)
+
     high, low, own = pl.ds(PADC, 8), pl.ds(56, 8), pl.ds(0, PADC)
     part_plan = (
-        (total.at[inner, low], part_right, la, left),
-        (total.at[inner, high], part_left, la, right),
+        (send_low, part_right, la, left),
+        (send_high, part_left, la, right),
         (total.at[0, own], part_bottom, up, lo),
         (total.at[ROWS + 1, own], part_top, down, lo),
         (total.at[0, low], part_corner.at[0], up, left),
@@ -433,32 +439,36 @@
     stores.append(pltpu.make_async_copy(final, weight_sum.at[plane_rank], store_sem.at[2]))
     stores[1].start()
 
+    for copy in halos:
+        copy.wait_send()
     for copy in parts:
         copy.wait_recv()
     for copy in parts:
         copy.wait_send()
 
-    part_left[0] += part_corner[3]
-    part_right[0] += part_corner[2]
-    part_left[ROWS - 1] += part_corner[1]
-    part_right[ROWS - 1] += part_corner[0]
+    def at_end(strip):
+        return pltpu.roll(jnp.concatenate([strip, jnp.zeros((8, CHAN), F32)], axis=0), 5, 0)
+
     total[1, 0:PADC] += part_top[...]
     total[ROWS, 0:PADC] += part_bottom[...]
-
-    @pl.loop(0, ROWS, unroll=2)
-    def _(i):
-        after = pltpu.roll(
-            jnp.concatenate([part_right[i], jnp.zeros((8, CHAN), F32)], axis=0), 5, 0
-        )
-        extra = jnp.concatenate([part_left[i], jnp.zeros((24, CHAN), F32), after], axis=0)
-        result = (total[i + 1, 0:PADC] + extra) * seen[i + 1, 0:PADC].astype(F32)
-        spill(wide_feat, i, result)
+    for i, first, last in ((1, 3, 2), (ROWS, 1, 0)):
+        total[i, 0:8] += part_corner[first]
+        total[i, 32:PADC] += at_end(part_corner[last])
+
+    @pl.loop(0, PAIRS, unroll=2)
+    def _(t):
+        before, after = part_left[t].astype(F32), part_right[t].astype(F32)
+        for k in range(2):
+            i, rows = 2 * t + k, slice(8 * k, 8 * k + 8)
+            extra = jnp.concatenate(
+                [before[rows], jnp.zeros((24, CHAN), F32), at_end(after[rows])], axis=0
+            )
+            result = (total[i + 1, 0:PADC] + extra) * seen[i + 1, 0:PADC].astype(F32)
+            spill(wide_feat, i, result)
 
     narrow(wide_feat, feat_own)
     stores.append(pltpu.make_async_copy(feat_own, input_grad, store_sem.at[1]))
     stores[2].start()
-    for copy in halos:
-        copy.wait_send()
 
     for copy in gathers + swaps:
         copy.wait_send()
@@ -505,6 +515,7 @@
     n_lat, n_lon = lax.axis_size("lat"), lax.axis_size("lon")
     anywhere = pl.BlockSpec(memory_space=pltpu.HBM)
     marks = pltpu.VMEM((16, ROWS * GROUPS), BF16)
+    strips = pltpu.VMEM((PAIRS, 16, CHAN), BF16)
     field = jax.ShapeDtypeStruct((COLS, ROWS, CHAN), BF16)
     infilled, input_grad, sums = pl.pallas_call(
         functools.partial(kernel, n_lat, n_lon),
@@ -546,8 +557,7 @@
             pltpu.VMEM((15, 8, CHAN), F32),
             pltpu.VMEM((16, 8, CHAN), F32),
             pltpu.VMEM((8, CHAN), F32),
-            pltpu.VMEM((ROWS, 8, CHAN), F32),
-            pltpu.VMEM((ROWS, 8, CHAN), F32),
+            strips, strips, strips, strips,
             pltpu.VMEM((PADC, CHAN), F32),
             pltpu.VMEM((PADC, CHAN), F32),
             pltpu.VMEM((4, 8, CHAN), F32),

time: 42.1 us -> 40.4 us (0.960)
  Pallas kernels: 41.4 us -> 39.6 us
    pallas_call x1, Pallas kernels: 39 us -> 37.2 us  [local(): pl.pallas_call(functools.partial(kernel, n_lat, n_lon), out_shape=(field,...]
where the time goes in v4:
time: 40.4 us; the launch traced here: 40.3 us
  Pallas kernels  39.6 us (98%)
  between operations  0.64 us (2%)
    pallas_call x1, Pallas kernels, local(): pl.pallas_call(functools.partial(kernel, n_lat, n_lon), out_shape=(field,...  37.2 us
    pallas_call x1, Pallas kernels, local(): pl.pallas_call(finish, out_shape=(jax.ShapeDtypeStruct((GROUPS, BASES, WI...  2.38 us

profile of v4, /device:TPU:1, one launch (start us, length us, event | category | flops | bytes accessed | tf_op | source)
XLA Modules:
  0.0 40.3 jit_solution(1265144458779743346)
XLA Ops:
  0.6 37.2 %shard_map.85 = (bf16[45,24,256]{2,1,0:T(8,128)(2,1)}, bf16[45,24,256]{2,1,0:T(8,128)(2,1)}, f32[16,8,256]{2,1,0:T(8,128)}) custom-call(bf16[45,24,256]{2,1,0:T(8,128)(2,1)} %bitcast.6, s32[24,8,45]{2,1,0:T(8,128)} %bitcast.9, bf16[3,17,4,384]{3,2,1,0:T(4,128)(2,1)} %bitcast.8, s32[384]{0:T(512)} %width.1, bf16[8,4,32,32]{3,2,1,0:T(8,128)(2,1)} %mix.1, ...), custom_call_target="tpu_custom_call" | custom-call | tf_op jit(solution)/shard_map/pallas_call | solution.py:520
  37.9 2.4 %shard_map.86 = (f32[8,4,32,32]{3,2,1,0:T(8,128)}, bf16[45,24,256]{2,1,0:T(8,128)(2,1)}, bf16[45,24,256]{2,1,0:T(8,128)(2,1)}) custom-call(f32[16,8,256]{2,1,0:T(8,128)} %get-tuple-element.9.sums, bf16[45,24,256]{2,1,0:T(8,128)(2,1)} %get-tuple-element.10.first, bf16[45,24,256]{2,1,0:T(8,128)(2,1)} %get-tuple-element.11.second), custom_call_target="tpu_custom_call" | custom-call | tf_op jit(solution)/shard_map/pallas_call | solution.py:584

commit v5 on v4

--- a/solution.py
+++ b/solution.py
@@ -334,10 +334,6 @@
                 scaled[b, pl.ds(start, PADC)] = normal[first : first + PADC]
         pulled[t] = (back[t] * shrink).astype(BF16)
 
-    for b in range(BASES):
-        grad = jnp.where(block, dot(cots_t[...], scaled[b]), 0.0)
-        share[b * WIDTH : b * WIDTH + WIDTH] = jnp.sum(grad.reshape(GROUPS, WIDTH, CHAN), axis=0)
-
     def gather_share(n):
         to, device = plane(PLANE[n])
         rows = pl.ds(pl.multiple_of(to * 8, 8), 8)
@@ -366,7 +362,16 @@
         for copy in copies:
             copy.wait_recv()
 
-    gathers = start_all(gather_share)
+    gathers = []
+    for away_y in (2, 1, 3, 0):
+        b = lax.rem(chip_y + away_y, BASES)
+        grad = jnp.where(block, dot(cots_t[...], scaled[b]), 0.0)
+        rows = pl.ds(pl.multiple_of(b * WIDTH, WIDTH), WIDTH)
+        share[rows] = jnp.sum(grad.reshape(GROUPS, WIDTH, CHAN), axis=0)
+        for n, step in enumerate(PLANE):
+            if step[0] == away_y:
+                gathers.append(gather_share(n))
+                gathers[-1].start()
 
     total[0:2] = jnp.zeros((2, SLOT, CHAN), F32)
 

time: 40.4 us -> 41 us (1.015)
  Pallas kernels: 39.6 us -> 40.2 us
    pallas_call x1, Pallas kernels: 37.2 us -> 37.9 us  [local(): pl.pallas_call(functools.partial(kernel, n_lat, n_lon), out_shape=(field,...]
where the time goes in v5:
time: 41 us; the launch traced here: 40.9 us
  Pallas kernels  40.2 us (98%)
  between operations  0.64 us (2%)
    pallas_call x1, Pallas kernels, local(): pl.pallas_call(functools.partial(kernel, n_lat, n_lon), out_shape=(field,...  37.9 us
    pallas_call x1, Pallas kernels, local(): pl.pallas_call(finish, out_shape=(jax.ShapeDtypeStruct((GROUPS, BASES, WI...  2.38 us

profile of v5, /device:TPU:1, one launch (start us, length us, event | category | flops | bytes accessed | tf_op | source)
XLA Modules:
  0.0 40.9 jit_solution(13665075725456657539)
XLA Ops:
  0.6 37.9 %shard_map.85 = (bf16[45,24,256]{2,1,0:T(8,128)(2,1)}, bf16[45,24,256]{2,1,0:T(8,128)(2,1)}, f32[16,8,256]{2,1,0:T(8,128)}) custom-call(bf16[45,24,256]{2,1,0:T(8,128)(2,1)} %bitcast.6, s32[24,8,45]{2,1,0:T(8,128)} %bitcast.9, bf16[3,17,4,384]{3,2,1,0:T(4,128)(2,1)} %bitcast.8, s32[384]{0:T(512)} %width.1, bf16[8,4,32,32]{3,2,1,0:T(8,128)(2,1)} %mix.1, ...), custom_call_target="tpu_custom_call" | custom-call | tf_op jit(solution)/shard_map/pallas_call | solution.py:525
  38.5 2.4 %shard_map.86 = (f32[8,4,32,32]{3,2,1,0:T(8,128)}, bf16[45,24,256]{2,1,0:T(8,128)(2,1)}, bf16[45,24,256]{2,1,0:T(8,128)(2,1)}) custom-call(f32[16,8,256]{2,1,0:T(8,128)} %get-tuple-element.9.sums, bf16[45,24,256]{2,1,0:T(8,128)(2,1)} %get-tuple-element.10.first, bf16[45,24,256]{2,1,0:T(8,128)(2,1)} %get-tuple-element.11.second), custom_call_target="tpu_custom_call" | custom-call | tf_op jit(solution)/shard_map/pallas_call | solution.py:589
